TPU v7x, 512 devices: a whole 4x4x16 slice. The times are simulated.
512 devices in a mesh: dp: 64 (over x, z_hi, y), tensor: 8 (over z_lo, core).
Axes of the slice: x: 4, y: 4, z: 16 (z_hi: 4, z_lo: 4; z = z_hi * 4 + z_lo), core: 2. Of those that a mesh axis runs over, the one named last changes fastest.
Arguments:
- inputs: bfloat16 [32768, 6144], P('dp', 'tensor'), may hold values from -16 to 16
- expert_ids: int32 [32768, 2], P('dp'), may hold values from 0 to 7, as said below
- hidden_grads: bfloat16 [32768, 2, 16384], P('dp', None, 'tensor'), may hold values from -42 to 42
- input_probes: bfloat16 [6144, 48], P('tensor'), may hold values from -6 to 6
- hidden_probes: bfloat16 [16384, 32], P('tensor'), may hold values from -6 to 6
Outputs:
- input_sketch: float32 [6144, 384], P(('tensor', 'dp'))
- hidden_sketch: float32 [16384, 256], P(('tensor', 'dp'))
Inputs may be any that keep to these rules, and one draw needn't show every extreme that they name: `expert_ids`: the 2 experts of a token differ; every expert is named by some token.
All inputs are finite; a program needn't handle non-finite values.
Results may differ from a plain program's by a relative error of at most 0.0024.
Values sent between devices are 32-bit elements; how exact they have to be, the bound alone decides.
No kernel may reach another device: no remote copies, remote signals or barrier semaphores. Data moves between devices by JAX's collectives and lax.ppermute only.
A program may use at most 64 MiB of HBM per device.

v0:
```python
import math

import jax
import jax.numpy as jnp
from jax import lax
from jax.sharding import PartitionSpec as P

FF = 16384
EXPERTS = 8
PROBES = 48
HPROBES = 32


EPS = 1e-06


def contract(left, right):
    return lax.dot_general(
        left, right, (((0,), (0,)), ((), ())), preferred_element_type=jnp.float32
    )


def body(inputs, expert_ids, hidden_grads, input_probes, hidden_probes):
    tokens = inputs.shape[0]
    top_count = expert_ids.shape[1]
    width = hidden_grads.shape[2]
    experts = jnp.arange(EXPERTS, dtype=jnp.int32)
    onehot = (expert_ids[:, :, None] == experts).astype(jnp.int32)
    routed = jnp.sum(onehot, axis=1)
    counts = lax.psum(jnp.sum(routed, axis=0), "dp").astype(jnp.float32)
    grads_wide = hidden_grads.astype(jnp.float32)
    local_squares = jnp.sum(grads_wide * grads_wide, axis=2)
    partial_proj = jnp.dot(inputs, input_probes, preferred_element_type=jnp.float32)
    squares, projected = lax.psum((local_squares, partial_proj), "tensor")
    weighted = (routed.astype(jnp.float32)[:, :, None] * projected[:, None, :]).astype(jnp.bfloat16)
    weighted = weighted.reshape(tokens, EXPERTS * PROBES)
    scale = jnp.minimum(1.0, math.sqrt(FF) * lax.rsqrt(squares + EPS))
    clipped = (grads_wide * scale[:, :, None]).astype(jnp.bfloat16)
    flat = clipped.reshape(tokens * top_count, width)
    route_flat = onehot.reshape(tokens * top_count, EXPERTS).astype(jnp.float32)
    hprojected = jnp.dot(flat, hidden_probes, preferred_element_type=jnp.float32)
    hweighted = (route_flat[:, :, None] * hprojected[:, None, :]).astype(jnp.bfloat16)
    hweighted = hweighted.reshape(tokens * top_count, EXPERTS * HPROBES)
    input_sketch = lax.psum_scatter(
        contract(inputs, weighted), "dp", scatter_dimension=0, tiled=True
    )
    hidden_sketch = lax.psum_scatter(
        contract(flat, hweighted), "dp", scatter_dimension=0, tiled=True
    )
    input_scale = jnp.repeat(counts, PROBES)[None, :]
    hidden_scale = jnp.repeat(counts, HPROBES)[None, :]
    return (input_sketch / input_scale, hidden_sketch / hidden_scale)


def solution(mesh):
    return jax.shard_map(
        body,
        mesh=mesh,
        in_specs=(
            P("dp", "tensor"),
            P("dp", None),
            P("dp", None, "tensor"),
            P("tensor", None),
            P("tensor", None),
        ),
        out_specs=(P(("tensor", "dp"), None), P(("tensor", "dp"), None)),
        check_vma=False,
    )
```

profile of v0, /device:TPU:32, one launch (start us, length us, event | category | flops | bytes accessed | tf_op | source)
XLA Modules:
  0.0 1368.5 jit_solution(8623785197244941658)
XLA Ops:
  7.2 0.0 copy-start
  7.2 0.0 all-reduce.4.cloned.1.call-start
  7.2 1.1 copy-done
  8.3 1.9 fusion.2
  10.2 0.0 all-reduce.4.cloned.1.call-update
  10.2 0.0 all-reduce.6.cloned.1.call-start
  10.2 6.6 fusion
  16.8 0.1 copy.22
  16.9 15.0 %psum.23 = f32[512,2]{0,1:T(2,128)S(1)} all-reduce(f32[512,2]{0,1:T(2,128)S(1)} %copy.22), channel_id=1, replica_groups=mesh['dp'=64,'tensor'=8] {'tensor'}, use_global_device_ids=true, to_apply=%region_6.0 | all-reduce | flops 1024 | bytes 8192 | tf_op jit(solution)/shard_map/psum | solution.py:34
  32.0 0.2 copy.23
  32.1 7.5 fusion.1
  39.6 0.0 copy-start.3
  39.6 7.3 reshape.61
  46.9 0.0 copy-done.3
  46.9 0.0 copy-start.2
  46.9 0.1 copy.24
  47.0 0.2 eq.29
  47.2 0.1 convert_reduce_fusion
  47.3 42.5 %all-reduce.4.cloned.1.call-done = f32[512,48]{0,1:T(8,128)} async-done(((f32[512,48]{0,1:T(8,128)}), f32[512,48]{0,1:T(8,128)}) %all-reduce.4.cloned.1.call-update) | async-done | bytes 98320 | tf_op jit(solution)/shard_map/psum | solution.py:34
  89.9 0.9 multiply_convert_fusion.1
  90.8 1.5 convolution_bitcast_fusion
  92.3 0.0 all-reduce.6.cloned.1.call-update
  92.4 0.2 reduce-scatter.3.cloned.1.call-start
  92.6 0.0 copy-start.1
  92.6 0.0 copy-done.2
  92.6 3.7 fusion.3
  96.3 0.1 multiply_convert_fusion
  96.4 0.0 copy-done.1
  96.4 2.7 fusion.4
  99.1 0.0 reduce-scatter.3.cloned.1.call-update
  99.2 30.3 %psum.22 = s32[8]{0:T(128)S(1)} all-reduce(s32[8]{0:T(128)S(1)} %get-tuple-element.14), channel_id=1, replica_groups=mesh['dp'=64,'tensor'=8] {'dp'}, use_global_device_ids=true, to_apply=%region_4.0 | all-reduce | flops 8 | bytes 64 | tf_op jit(solution)/shard_map/psum | solution.py:30
  129.4 0.1 broadcast_in_dim.5
  129.5 0.1 div.23
  129.6 0.1 broadcast_in_dim.4
  129.7 0.1 div.20
  129.7 1.3 dynamic-slice
  131.7 784.2 %all-reduce.6.cloned.1.call-done = f32[768,384]{0,1:T(8,128)} async-done(((f32[768,384]{0,1:T(8,128)}), f32[768,384]{0,1:T(8,128)}) %all-reduce.6.cloned.1.call-update) | async-done | bytes 1179664
  915.8 1.2 dynamic-slice_divide_fusion
  917.0 0.7 copy.25
  917.7 442.9 %reduce-scatter.3.cloned.1.call-done = f32[32,256]{1,0:T(8,128)} async-done(((f32[2048,256]{1,0:T(8,128)}), f32[32,256]{1,0:T(8,128)}) %reduce-scatter.3.cloned.1.call-update) | async-done | bytes 32784 | tf_op jit(solution)/shard_map/reduce_scatter | solution.py:47
  1360.6 1.4 broadcast_divide_fusion
  (4 shorter events, 0.0 us)
Async XLA Ops:
  7.2 1.1 copy-start
  7.2 82.7 %all-reduce.4.cloned.1.call-start = ((), (), s32[]{:S(2)}) async-start(), calls=%async_computation.1 | async-start | bytes 196608 | tf_op jit(solution)/shard_map/psum | solution.py:34
  10.2 905.6 %all-reduce.6.cloned.1.call-start = ((), (), s32[]{:S(2)}) async-start(), calls=%async_computation.3 | async-start | bytes 2359296
  39.6 7.3 copy-start.3
  46.9 45.7 %copy-start.2 = (bf16[2048,32]{0,1:T(8,128)(2,1)S(1)}, bf16[2048,32]{0,1:T(8,128)(2,1)}, u32[]{:S(2)}) copy-start(bf16[2048,32]{0,1:T(8,128)(2,1)} %param.9) | copy-start | bytes 393220
  92.4 1268.2 %reduce-scatter.3.cloned.1.call-start = ((), (), s32[]{:S(2)}) async-start(), calls=%async_computation.2 | async-start | bytes 2129920 | tf_op jit(solution)/shard_map/reduce_scatter | solution.py:47
  92.6 3.8 copy-start.1
Sparse Core Ops, SparseCore 0:
  10.9 78.8 all-reduce.3
  93.0 822.7 all-reduce.5
  918.6 441.9 reduce-scatter.2
where the time goes:
time: 1370 us
  waiting for transfers between devices  1270 us (93%)
  blocking collectives  45.3 us (3%)
  other arithmetic  17.8 us (1%)
  between operations  14.5 us (1%)
    unnamed x4, waiting for transfers between devices  784 us
    reduce_scatter x1, waiting for transfers between devices, body(): lax.psum_scatter(contract(flat, hweighted), 'dp', scatter_dimension=0, ti...  443 us
    psum x1, waiting for transfers between devices, body(): squares, projected = lax.psum((local_squares, partial_proj), 'tensor')  42.5 us
    psum x1, blocking collectives, body(): counts = lax.psum(jnp.sum(routed, axis=0), 'dp').astype(jnp.float32)  30.3 us
  transfers between devices with their start and end apart: 3, of which 3 were waited for; matrix products, arithmetic and copies ran while one was open for 2% of the time, Pallas kernels for 0%

commit v1 on v0

v1 whole, which is shorter than its diff:
```python
import jax
import jax.numpy as jnp
from jax import lax
from jax.sharding import PartitionSpec as P

FF = 16384
EXPERTS = 8
PROBES = 48
HPROBES = 32
EPS = 1e-06
AXES = ("dp", "tensor")


def linear(x, zh, y, t):
    return ((x * 4 + zh) * 4 + y) * 8 + t


def ring_groups(first):
    groups = []
    for zh in range(4):
        for t in range(8):
            along_x = (t % 2 == 0) == first
            for other in range(4):
                groups.append(
                    [linear(i, zh, other, t) if along_x else linear(other, zh, i, t) for i in range(4)]
                )
    return groups


def zh_groups():
    return [
        [linear(x, zh, y, t) for zh in range(4)] for x in range(4) for y in range(4) for t in range(8)
    ]


def exchange(block, groups):
    got = lax.all_to_all(block, AXES, 0, 0, axis_index_groups=groups)
    return jnp.sum(got, axis=0)


def contract(left, right, dims):
    return lax.dot_general(left, right, (dims, ((), ())), preferred_element_type=jnp.float32)


def body(inputs, expert_ids, hidden_grads, input_probes, hidden_probes):
    tokens = inputs.shape[0]
    width = hidden_grads.shape[2]
    experts = jnp.arange(EXPERTS, dtype=jnp.int32)
    onehot = (expert_ids[:, :, None] == experts).astype(jnp.float32)
    routed = jnp.sum(onehot, axis=1)
    local_counts = jnp.sum(routed, axis=0)

    grads_wide = hidden_grads.astype(jnp.float32)
    local_squares = jnp.sum(grads_wide * grads_wide, axis=2)
    partial_proj = contract(input_probes, inputs, ((0,), (1,)))
    hproj = contract(hidden_grads, hidden_probes, ((2,), (0,)))

    send = jnp.concatenate(
        [
            partial_proj.reshape(8, 6, tokens),
            jnp.broadcast_to(local_squares.T[None], (8, 2, tokens)),
        ],
        axis=1,
    )
    mine = jnp.sum(lax.all_to_all(send, "tensor", 0, 0), axis=0)
    squares = mine[6:].T
    everyone = lax.all_to_all(jnp.broadcast_to(mine[None], (8, 8, tokens)), "tensor", 0, 0)
    projected = everyone[:, :6].reshape(PROBES, tokens).T

    weighted = (routed[:, :, None] * projected[:, None, :]).astype(jnp.bfloat16)
    weighted = weighted.reshape(tokens, EXPERTS * PROBES)
    square_scale = jnp.minimum(1.0, FF / (squares + EPS))
    hweighted = (onehot[:, :, :, None] * (square_scale[:, :, None] * hproj)[:, :, None, :]).astype(
        jnp.bfloat16
    )
    hweighted = hweighted.reshape(tokens, 2, EXPERTS * HPROBES)
    hidden = contract(hidden_grads, hweighted, ((0, 1), (0, 1)))
    inp = contract(inputs, weighted, ((0,), (0,)))

    hidden = hidden.reshape(64, width // 64, 2, 128).transpose(0, 2, 1, 3).reshape(64, 64, 128)
    inp = inp.reshape(64, 12, 3, 128).transpose(0, 2, 1, 3).reshape(64, 36, 128)
    count_rows = jnp.broadcast_to(jnp.pad(local_counts, (0, 120)), (64, 4, 128))
    block = jnp.concatenate([hidden, inp, count_rows], axis=1).reshape(4, 4, 4, 104, 128)
    even = lax.axis_index("tensor") % 2 == 0
    block = jnp.where(even, block.transpose(0, 2, 1, 3, 4), block.transpose(2, 0, 1, 3, 4))
    block = exchange(block, ring_groups(True))
    block = exchange(block, ring_groups(False))
    block = exchange(block, zh_groups())

    counts = block[100, :8]
    hidden = jnp.concatenate([block[:32], block[32:64]], axis=1)
    inp = jnp.concatenate([block[64:76], block[76:88], block[88:100]], axis=1)
    return (
        inp / jnp.repeat(counts, PROBES)[None, :],
        hidden / jnp.repeat(counts, HPROBES)[None, :],
    )


def solution(mesh):
    return jax.shard_map(
        body,
        mesh=mesh,
        in_specs=(
            P("dp", "tensor"),
            P("dp", None),
            P("dp", None, "tensor"),
            P("tensor", None),
            P("tensor", None),
        ),
        out_specs=(P(("tensor", "dp"), None), P(("tensor", "dp"), None)),
        check_vma=False,
    )
```

time: 1370 us -> 127 us (0.09)
  waiting for transfers between devices: 1270 us -> 5.56 us
  blocking collectives: 45.3 us -> 68.8 us
    unnamed x4 -> x0, waiting for transfers between devices: 784 us -> none
    reduce_scatter x1 -> x0, waiting for transfers between devices: 443 us -> none  [body(): lax.psum_scatter(contract(flat, hweighted), 'dp', scatter_dimension=0, ti...]
    all_to_all x0 -> x3, blocking collectives: none -> 68.8 us  [exchange(): got = lax.all_to_all(block, AXES, 0, 0, axis_index_groups=groups)]
    psum x2 -> x0, blocking collectives: 45.3 us -> none  [the longest x1 30.3 us: body(): counts = lax.psum(jnp.sum(routed, axis=0), 'dp').astype(jnp.float32)]
    psum x1 -> x0, waiting for transfers between devices: 42.5 us -> none  [body(): squares, projected = lax.psum((local_squares, partial_proj), 'tensor')]
  transfers between devices with their start and end apart: 3 -> 2, of which waited for: 3 -> 1; matrix products, arithmetic and copies ran while one was open for 2% -> 12% of each run, Pallas kernels for 0% -> 0%
where the time goes in v1:
time: 127 us; the launch traced here: 126 us
  blocking collectives  68.8 us (54%)
  local copies, waits for them, and re-layouts  15.4 us (12%)
  starting transfers between devices  13.2 us (10%)
  other arithmetic  11.7 us (9%)
  matrix products  10.7 us (8%)
  waiting for transfers between devices  5.56 us (4%)
    all_to_all x3, blocking collectives, exchange(): got = lax.all_to_all(block, AXES, 0, 0, axis_index_groups=groups)  68.8 us
    dot_general x4, matrix products, contract(): lax.dot_general(left, right, (dims, ((), ())), preferred_element_type=jnp...  10.7 us
    all_to_all x1, starting transfers between devices, body(): mine = jnp.sum(lax.all_to_all(send, 'tensor', 0, 0), axis=0)  8.76 us
    reduce_sum x1, other arithmetic, body(): local_squares = jnp.sum(grads_wide * grads_wide, axis=2)  6.67 us
    all_to_all x1, waiting for transfers between devices, body(): mine = jnp.sum(lax.all_to_all(send, 'tensor', 0, 0), axis=0)  5.56 us
    dot_general x2, local copies, waits for them, and re-layouts, contract(): lax.dot_general(left, right, (dims, ((), ())), preferred_element_type=jnp...  4.58 us
    all_to_all x1, starting transfers between devices, body(): lax.all_to_all(jnp.broadcast_to(mine[None], (8, 8, tokens)), 'tensor', 0, 0)  4.39 us
    reshape x1, local copies, waits for them, and re-layouts, body(): inp = inp.reshape(64, 12, 3, 128).transpose(0, 2, 1, 3).reshape(64, 36, 128)  2.78 us
  transfers between devices with their start and end apart: 2, of which 1 were waited for; matrix products, arithmetic and copies ran while one was open for 12% of the time, Pallas kernels for 0%

profile of v1, /device:TPU:32, one launch (start us, length us, event | category | flops | bytes accessed | tf_op | source)
XLA Modules:
  0.0 126.2 jit_solution(2695090325075767974)
XLA Ops:
  0.6 0.0 copy-start
  0.6 0.0 copy-start.2
  0.7 0.0 copy-start.3
  0.7 0.0 copy-start.4
  0.7 6.7 %multiply_reduce_fusion = f32[512,2]{1,0:T(8,128)S(1)} fusion(bf16[512,2,2048]{2,1,0:T(2,128)(2,1)} %param.7), kind=kLoop, calls=%fused_computation | loop fusion | flops 6290432 | bytes 4198400 | tf_op jit(solution)/shard_map/reduce_sum | solution.py:54
  7.3 0.1 copy.29
  7.5 0.0 copy-done
  7.5 0.0 copy-done.2
  7.5 0.3 fusion.19
  7.9 0.7 pad_maximum_fusion.1
  8.5 8.8 %all-to-all-start = ((f32[8,8,512]{2,1,0:T(8,128)}), f32[8,8,512]{2,1,0:T(8,128)S(1)}, u32[]{:S(2)}, u32[]{:S(2)}) async-start(f32[8,8,512]{2,1,0:T(8,128)} %pad_maximum_fusion.1), calls=%async_computation | async-start | bytes 262144 | tf_op jit(solution)/shard_map/all_to_all | solution.py:65
  17.3 0.0 copy-done.3
  17.3 0.1 fusion.13
  17.4 5.6 %all-to-all-done = f32[8,8,512]{2,1,0:T(8,128)S(1)} async-done(((f32[8,8,512]{2,1,0:T(8,128)}), f32[8,8,512]{2,1,0:T(8,128)S(1)}, u32[]{:S(2)}, u32[]{:S(2)}) %all-to-all-start) | async-done | bytes 131104 | tf_op jit(solution)/shard_map/all_to_all | solution.py:65
  23.0 0.7 broadcast_in_dim.11
  23.7 4.4 %all-to-all-start.1 = ((f32[8,8,512]{2,1,0:T(8,128)}), f32[8,8,512]{2,1,0:T(8,128)S(1)}, u32[]{:S(2)}, u32[]{:S(2)}) async-start(f32[8,8,512]{2,1,0:T(8,128)} %broadcast_in_dim.11), calls=%async_computation.1 | async-start | bytes 262144 | tf_op jit(solution)/shard_map/all_to_all | solution.py:67
  28.1 0.0 copy-done.4
  28.1 0.0 copy-start.1
  28.1 4.7 %fusion.7 = f32[512,2,32]{0,2,1:T(8,128)S(1)} fusion(bf16[512,2,2048]{2,1,0:T(2,128)(2,1)} %param.7, bf16[2048,32]{0,1:T(8,128)(2,1)S(1)} %copy-done.4, f32[512,2]{0,1:T(2,128)S(1)} %fusion.16), kind=kOutput, calls=%fused_computation.9 | convolution fusion | flops 134250496 | bytes 4460544 | tf_op jit(solution)/shard_map/dot_general | solution.py:42
  32.8 0.1 multiply_convert_fusion
  32.9 0.0 copy-done.1
  32.9 4.2 %fusion.4 = f32[2048,256]{0,1:T(8,128)} fusion(bf16[512,2,256]{0,2,1:T(8,128)(2,1)S(1)} %bitcast.38, bf16[512,2,2048]{2,1,0:T(2,128)(2,1)S(1)} %copy-done.1), kind=kOutput, calls=%fused_computation.7 | convolution fusion | flops 1073741824 | bytes 6815744 | tf_op jit(solution)/shard_map/dot_general | solution.py:42
  37.1 1.9 %copy.32 = f32[2048,256]{1,0:T(8,128)S(1)} copy(f32[2048,256]{0,1:T(8,128)} %fusion.4) | data formatting | bytes 4194304 | tf_op jit(solution)/shard_map/dot_general | solution.py:42
  39.0 2.1 %reshape.48 = f32[64,32,2,128]{3,2,1,0:T(2,128)} reshape(f32[2048,256]{1,0:T(8,128)S(1)} %copy.32) | data formatting | bytes 4194304 | tf_op jit(solution)/shard_map/reshape | solution.py:80
  41.2 1.8 %copy.33 = f32[64,2,32,128]{3,2,1,0:T(8,128)S(1)} copy(f32[64,2,32,128]{3,1,2,0:T(2,128)} %bitcast.32) | data formatting | bytes 4194304 | tf_op jit(solution)/shard_map/transpose | solution.py:80
  43.0 0.0 all-to-all-done.1
  43.1 1.5 %convolution_bitcast_fusion = f32[768,384]{0,1:T(8,128)} fusion(bf16[512,384]{0,1:T(8,128)(2,1)S(1)} %bitcast.35, bf16[512,768]{1,0:T(8,128)(2,1)S(1)} %copy-done), kind=kOutput, calls=%fused_computation.8 | convolution fusion | flops 301989888 | bytes 2359296 | tf_op jit(solution)/shard_map/dot_general | solution.py:42
  44.6 2.7 %copy.34 = f32[768,384]{1,0:T(8,128)} copy(f32[768,384]{0,1:T(8,128)} %convolution_bitcast_fusion) | data formatting | bytes 2359296 | tf_op jit(solution)/shard_map/dot_general | solution.py:42
  47.3 2.8 %reshape.50 = f32[64,12,3,128]{3,2,1,0:T(4,128)} reshape(f32[768,384]{1,0:T(8,128)} %copy.34) | data formatting | bytes 2359296 | tf_op jit(solution)/shard_map/reshape | solution.py:81
  50.0 1.8 %copy.35 = f32[64,3,12,128]{3,0,2,1:T(8,128)S(1)} copy(f32[64,3,12,128]{3,1,2,0:T(4,128)} %bitcast.33) | data formatting | bytes 2359296 | tf_op jit(solution)/shard_map/transpose | solution.py:81
  51.8 0.7 copy.36
  52.5 0.3 pad_maximum_fusion
  52.9 0.3 bitcast_select_fusion
  53.1 0.4 copy.38
  53.5 26.9 %all_to_all.25 = f32[4,4,4,104,128]{4,3,2,1,0:T(8,128)} all-to-all(f32[4,4,4,104,128]{4,3,2,1,0:T(8,128)S(1)} %copy.38), channel_id=1, replica_groups={{0,128,256,384},{8,136,264,392},{16,144,272,400},{24,152,280,408},{1,9,..., dimensions={0} | all-to-all | bytes 6815744 | tf_op jit(solution)/shard_map/all_to_all | solution.py:37
  80.4 2.2 %reduce_sum.67 = f32[4,4,104,128]{3,2,1,0:T(8,128)S(1)} reduce(f32[4,4,4,104,128]{4,3,2,1,0:T(8,128)} %all_to_all.25, f32[]{:T(128)} %constant.24.clone.1), dimensions={0}, to_apply=%region_4.5 | reduce | flops 638976 | bytes 4259844 | tf_op jit(solution)/shard_map/reduce_sum | solution.py:38
  82.6 12.2 %all_to_all.26 = f32[4,4,104,128]{3,2,1,0:T(8,128)S(1)} all-to-all(f32[4,4,104,128]{3,2,1,0:T(8,128)S(1)} %reduce_sum.67), channel_id=1, replica_groups={{0,8,16,24},{128,136,144,152},{256,264,272,280},{384,392,400,408},{1,12..., dimensions={0} | all-to-all | bytes 1703936 | tf_op jit(solution)/shard_map/all_to_all | solution.py:37
  94.9 29.7 %all_to_all.27 = f32[4,104,128]{2,1,0:T(8,128)S(1)} all-to-all(f32[4,104,128]{2,1,0:T(8,128)S(1)} %reduce_sum.68), channel_id=1, replica_groups={{0,32,64,96},{1,33,65,97},{2,34,66,98},{3,35,67,99},{4,36,68,100},{5,37..., dimensions={0} | all-to-all | bytes 425984 | tf_op jit(solution)/shard_map/all_to_all | solution.py:37
  124.7 0.1 broadcast_in_dim.13
  124.7 0.1 div.29
  124.8 0.1 broadcast_in_dim.14
  124.9 0.1 div.32
  125.0 0.6 maximum_divide_fusion
  125.6 0.6 maximum_divide_fusion.1
  (14 shorter events, 0.2 us)
Async XLA Ops:
  0.6 6.8 %copy-start = (bf16[512,768]{1,0:T(8,128)(2,1)S(1)}, bf16[512,768]{1,0:T(8,128)(2,1)}, u32[]{:S(2)}) copy-start(bf16[512,768]{1,0:T(8,128)(2,1)} %param.5) | copy-start | bytes 2359300
  0.6 6.8 %copy-start.2 = (bf16[768,48]{0,1:T(8,128)(2,1)S(1)}, bf16[768,48]{0,1:T(8,128)(2,1)}, u32[]{:S(2)}) copy-start(bf16[768,48]{0,1:T(8,128)(2,1)} %param.8) | copy-start | bytes 221188
  0.7 16.6 %copy-start.3 = (s32[512,2]{0,1:T(2,128)S(1)}, s32[512,2]{0,1:T(2,128)}, u32[]{:S(2)}) copy-start(s32[512,2]{0,1:T(2,128)} %param.6) | copy-start | bytes 12292
  0.7 27.4 %copy-start.4 = (bf16[2048,32]{0,1:T(8,128)(2,1)S(1)}, bf16[2048,32]{0,1:T(8,128)(2,1)}, u32[]{:S(2)}) copy-start(bf16[2048,32]{0,1:T(8,128)(2,1)} %param.9) | copy-start | bytes 393220
  8.5 14.5 %all-to-all-start = ((f32[8,8,512]{2,1,0:T(8,128)}), f32[8,8,512]{2,1,0:T(8,128)S(1)}, u32[]{:S(2)}, u32[]{:S(2)}) async-start(f32[8,8,512]{2,1,0:T(8,128)} %pad_maximum_fusion.1), calls=%async_computation | async-start | bytes 262144 | tf_op jit(solution)/shard_map/all_to_all | solution.py:65
  23.7 19.3 %all-to-all-start.1 = ((f32[8,8,512]{2,1,0:T(8,128)}), f32[8,8,512]{2,1,0:T(8,128)S(1)}, u32[]{:S(2)}, u32[]{:S(2)}) async-start(f32[8,8,512]{2,1,0:T(8,128)} %broadcast_in_dim.11), calls=%async_computation.1 | async-start | bytes 262144 | tf_op jit(solution)/shard_map/all_to_all | solution.py:67
  28.1 4.8 %copy-start.1 = (bf16[512,2,2048]{2,1,0:T(2,128)(2,1)S(1)}, bf16[512,2,2048]{2,1,0:T(2,128)(2,1)}, u32[]{:S(2)}) copy-start(bf16[512,2,2048]{2,1,0:T(2,128)(2,1)} %param.7) | copy-start | bytes 12582916

commit v2 on v1

v2 whole, which is shorter than its diff:
```python
import functools

import jax
import jax.numpy as jnp
from jax import lax
from jax.experimental import pallas as pl
from jax.experimental.pallas import tpu as pltpu
from jax.sharding import PartitionSpec as P

FF = 16384
EXPERTS = 8
PROBES = 48
HPROBES = 32
EPS = 1e-06
AXES = ("dp", "tensor")
PARAMS = pltpu.CompilerParams(vmem_limit_bytes=40 * 1024 * 1024)
VMEM = pl.BlockSpec(memory_space=pltpu.VMEM)
SMEM = pl.BlockSpec(memory_space=pltpu.SMEM)


def linear(x, zh, y, t):
    return ((x * 4 + zh) * 4 + y) * 8 + t


def ring_groups(first):
    groups = []
    for zh in range(4):
        for t in range(8):
            along_x = (t % 2 == 0) == first
            for other in range(4):
                groups.append(
                    [linear(i, zh, other, t) if along_x else linear(other, zh, i, t) for i in range(4)]
                )
    return groups


def zh_groups():
    return [
        [linear(x, zh, y, t) for zh in range(4)] for x in range(4) for y in range(4) for t in range(8)
    ]


def swap(block, groups):
    return lax.all_to_all(block, AXES, 0, 0, axis_index_groups=groups)


def nt(left, right, **kw):
    return lax.dot_general(
        left, right, (((1,), (1,)), ((), ())), preferred_element_type=jnp.float32, **kw
    )


def first_kernel(grads_ref, inputs_ref, hprobes_ref, probes_ref, send_ref, hproj_ref):
    ones = jnp.ones((8, 128), jnp.float32)
    for b in range(4):
        rows = grads_ref[256 * b : 256 * (b + 1)]
        wide = rows.astype(jnp.float32)
        part = jnp.zeros((256, 128), jnp.float32)
        for i in range(16):
            piece = wide[:, 128 * i : 128 * (i + 1)]
            part = part + piece * piece
        squares = nt(ones, part, precision=lax.Precision.HIGHEST)
        hproj_ref[:, 256 * b : 256 * (b + 1)] = nt(hprobes_ref[...], rows)
        proj = nt(probes_ref[...], inputs_ref[128 * b : 128 * (b + 1)])
        lanes = 256 * (b % 2)
        for t in range(8):
            send_ref[t, 0:6, 128 * b : 128 * (b + 1)] = proj[6 * t : 6 * t + 6]
            send_ref[t, 6 + b // 2, lanes : lanes + 256] = squares[0]


def hidden_kernel(place_ref, got_ref, hproj_ref, ids_ref, grads_ref, out_ref):
    got = jnp.sum(got_ref[...], axis=0)
    squares = jnp.concatenate([got[6:7], got[7:8]], axis=1)
    scaled = hproj_ref[...] * jnp.minimum(1.0, FF / (squares + EPS))
    ids = ids_ref[...]
    weights = jnp.concatenate(
        [jnp.where(ids == e, scaled, 0.0).astype(jnp.bfloat16) for e in range(EXPERTS)], axis=0
    )
    rows = grads_ref[...]
    for b in range(8):
        product = jnp.dot(
            weights, rows[:, 256 * b : 256 * (b + 1)], preferred_element_type=jnp.float32
        ).T
        for c in range(8):
            out_ref[place_ref[8 * b + c]] = product[32 * c : 32 * c + 32]


def input_kernel(core_ref, everyone_ref, ids_ref, inputs_ref, out_ref):
    projected = jnp.concatenate([everyone_ref[t, 0:6] for t in range(8)], axis=0)
    ids = ids_ref[...]
    routed = [(ids[0:1] == e) | (ids[1:2] == e) for e in range(EXPERTS)]
    weights = jnp.concatenate(
        [jnp.where(r, projected, 0.0).astype(jnp.bfloat16) for r in routed], axis=0
    )
    product = jnp.dot(weights, inputs_ref[...], preferred_element_type=jnp.float32).T

    def marks(repeat, total):
        marked = [
            jnp.broadcast_to(jnp.where(r, 1.0, 0.0).astype(jnp.bfloat16), (repeat, r.shape[1]))
            for r in routed
        ]
        marked = jnp.concatenate(marked, axis=0)
        return nt(jnp.ones((8, r_tokens), jnp.bfloat16), marked)

    r_tokens = ids.shape[1]
    for_inputs = marks(PROBES, 384)
    for_hidden = jnp.concatenate([marks(HPROBES, 256), jnp.zeros((8, 128), jnp.float32)], axis=1)
    counts = jnp.concatenate(
        [for_inputs[0:1], for_hidden[0:1], jnp.zeros((6, 384), jnp.float32)], axis=0
    )
    for i in range(4):
        out_ref[i, 192:200] = counts

    def write(order):
        for x in range(4):
            for zh in range(4):
                for y in range(4):
                    start = ((x * 4 + zh) * 4 + y) * 12
                    major, minor = (x, y) if order else (y, x)
                    at = minor * 48 + zh * 12
                    out_ref[major, at : at + 12] = product[start : start + 12]

    pl.when(core_ref[0] == 0)(functools.partial(write, True))
    pl.when(core_ref[0] == 1)(functools.partial(write, False))


def last_kernel(hidden_ref, input_ref, input_out, hidden_out):
    total = jnp.sum(input_ref[...], axis=0)
    input_out[...] = total[0:12] / total[12:13]
    hidden_out[...] = jnp.sum(hidden_ref[...], axis=0) / total[13:14, :256]


def call(kernel, out_shape, in_specs, out_specs, flops, size):
    return pl.pallas_call(
        kernel,
        out_shape=out_shape,
        in_specs=in_specs,
        out_specs=out_specs,
        compiler_params=PARAMS,
        cost_estimate=pl.CostEstimate(flops=flops, bytes_accessed=size, transcendentals=0),
    )


def shape(*dims):
    return jax.ShapeDtypeStruct(dims, jnp.float32)


def body(inputs, expert_ids, hidden_grads, input_probes, hidden_probes):
    tokens = inputs.shape[0]
    core = lax.axis_index("tensor") % 2
    dp = jnp.arange(64, dtype=jnp.int32)
    x, zh, y = dp // 16, dp // 4 % 4, dp % 4
    place = jnp.where(core == 0, (x * 4 + y) * 4 + zh, (y * 4 + x) * 4 + zh)
    ids_pair = expert_ids.T
    hidden_grads = hidden_grads.reshape(2 * tokens, -1)
    ids_row = expert_ids.reshape(1, 2 * tokens)

    send, hproj = call(
        first_kernel, (shape(8, 8, tokens), shape(HPROBES, 2 * tokens)), [VMEM] * 4, (VMEM, VMEM), 10**9, 5 * 10**6
    )(hidden_grads, inputs, hidden_probes.T, input_probes.T)
    got = lax.all_to_all(send, "tensor", 0, 0)
    hidden = call(
        hidden_kernel, shape(64, 32, 256), [SMEM] + [VMEM] * 4, VMEM, 10**9, 6 * 10**6
    )(place, got, hproj, ids_row, hidden_grads)
    hidden = swap(hidden.reshape(4, 16, 32, 256), ring_groups(True))

    mine = jnp.sum(got, axis=0)
    everyone = lax.all_to_all(jnp.broadcast_to(mine[None], (8, 8, tokens)), "tensor", 0, 0)
    inp = call(
        input_kernel, shape(4, 200, 384), [SMEM] + [VMEM] * 3, VMEM, 10**9, 3 * 10**6
    )(core.reshape(1), everyone, ids_pair, inputs)
    inp = swap(inp, ring_groups(True))

    hidden = swap(jnp.sum(hidden, axis=0).reshape(4, 4, 32, 256), ring_groups(False))
    inp = jnp.sum(inp, axis=0)
    counts = jnp.broadcast_to(inp[192:], (4, 8, 384))
    inp = swap(jnp.concatenate([inp[:192].reshape(4, 48, 384), counts], axis=1), ring_groups(False))

    hidden = swap(jnp.sum(hidden, axis=0), zh_groups())
    inp = jnp.sum(inp, axis=0)
    counts = jnp.broadcast_to(inp[48:52], (4, 4, 384))
    inp = swap(jnp.concatenate([inp[:48].reshape(4, 12, 384), counts], axis=1), zh_groups())
    return call(
        last_kernel, (shape(12, 384), shape(32, 256)), [VMEM] * 2, (VMEM, VMEM), 10**5, 10**5
    )(hidden, inp)


def solution(mesh):
    return jax.shard_map(
        body,
        mesh=mesh,
        in_specs=(
            P("dp", "tensor"),
            P("dp", None),
            P("dp", None, "tensor"),
            P("tensor", None),
            P("tensor", None),
        ),
        out_specs=(P(("tensor", "dp"), None), P(("tensor", "dp"), None)),
        check_vma=False,
    )
```

time: 127 us -> 140 us (1.10)
  waiting for transfers between devices: 5.56 us -> 51.3 us
  blocking collectives: 68.8 us -> 30.9 us
  starting transfers between devices: 13.2 us -> 30.6 us
  matrix products: 10.7 us -> 0 us
  other arithmetic: 11.7 us -> 3.26 us
  Pallas kernels: 0 us -> 8.07 us
    all_to_all x1 -> x5, waiting for transfers between devices: 5.56 us -> 45.6 us  [swap(): return lax.all_to_all(block, AXES, 0, 0, axis_index_groups=groups)]
    all_to_all x3 -> x2, blocking collectives: 68.8 us -> 30.9 us  [the longest x1 17.4 us: swap(): return lax.all_to_all(block, AXES, 0, 0, axis_index_groups=groups)]
    all_to_all x1 -> x5, starting transfers between devices: 8.76 us -> 26.2 us  [swap(): return lax.all_to_all(block, AXES, 0, 0, axis_index_groups=groups)]
    dot_general x4 -> x0, matrix products: 10.7 us -> none  [contract(): lax.dot_general(left, right, (dims, ((), ())), preferred_element_type=jnp...]
    pallas_call x0 -> x4, Pallas kernels: none -> 8.07 us  [the longest x1 3.26 us: body(): call(hidden_kernel, shape(64, 32, 256), [SMEM] + [VMEM] * 4, VMEM, 10 **...]
    reduce_sum x6 -> x5, other arithmetic: 9.1 us -> 1.85 us  [the longest x1 0.99 us: body(): jnp.sum(hidden, axis=0).reshape(4, 4, 32, 256)]
    all_to_all x1, waiting for transfers between devices: 0.01 us -> 5.7 us  [body(): lax.all_to_all(jnp.broadcast_to(mine[None], (8, 8, tokens)), 'tensor', 0, 0)]
    dot_general x2 -> x0, local copies, waits for them, and re-layouts: 4.58 us -> none  [contract(): lax.dot_general(left, right, (dims, ((), ())), preferred_element_type=jnp...]
  transfers between devices with their start and end apart: 2 -> 6, of which waited for: 1 -> 6; matrix products, arithmetic and copies ran while one was open for 12% -> 4% of each run, Pallas kernels for 0% -> 2%
where the time goes in v2:
time: 140 us; the launch traced here: 139 us
  waiting for transfers between devices  51.3 us (37%)
  blocking collectives  30.9 us (22%)
  starting transfers between devices  30.6 us (22%)
  local copies, waits for them, and re-layouts  14.3 us (10%)
  Pallas kernels  8.07 us (6%)
  other arithmetic  3.26 us (2%)
    all_to_all x5, waiting for transfers between devices, swap(): return lax.all_to_all(block, AXES, 0, 0, axis_index_groups=groups)  45.6 us
    all_to_all x5, starting transfers between devices, swap(): return lax.all_to_all(block, AXES, 0, 0, axis_index_groups=groups)  26.2 us
    all_to_all x1, blocking collectives, swap(): return lax.all_to_all(block, AXES, 0, 0, axis_index_groups=groups)  17.4 us
    all_to_all x1, blocking collectives, body(): got = lax.all_to_all(send, 'tensor', 0, 0)  13.6 us
    reshape x1, local copies, waits for them, and re-layouts, body(): hidden_grads = hidden_grads.reshape(2 * tokens, -1)  7.26 us
    all_to_all x1, waiting for transfers between devices, body(): lax.all_to_all(jnp.broadcast_to(mine[None], (8, 8, tokens)), 'tensor', 0, 0)  5.7 us
    unnamed x13, local copies, waits for them, and re-layouts  4.52 us
    all_to_all x1, starting transfers between devices, body(): lax.all_to_all(jnp.broadcast_to(mine[None], (8, 8, tokens)), 'tensor', 0, 0)  4.39 us
  transfers between devices with their start and end apart: 6, of which 6 were waited for; matrix products, arithmetic and copies ran while one was open for 4% of the time, Pallas kernels for 2%

profile of v2, /device:TPU:32, one launch (start us, length us, event | category | flops | bytes accessed | tf_op | source)
XLA Modules:
  0.0 139.3 jit_solution(16213453789837974446)
XLA Ops:
  0.6 0.0 copy-start.2
  0.6 0.0 copy-start.3
  0.7 0.0 copy-start.4
  0.7 7.3 %reshape.26.grads_ref = bf16[1024,2048]{1,0:T(8,128)(2,1)} reshape(bf16[512,2,2048]{2,1,0:T(2,128)(2,1)} %param.7) | data formatting | bytes 8388608 | tf_op jit(solution)/shard_map/reshape | solution.py:155
  7.9 0.0 copy-done.2
  7.9 0.0 copy-done.3
  7.9 0.0 copy-done.4
  7.9 0.0 copy-start
  7.9 2.2 %copy-done = bf16[1024,2048]{1,0:T(8,128)(2,1)S(1)} copy-done((bf16[1024,2048]{1,0:T(8,128)(2,1)S(1)}, bf16[1024,2048]{1,0:T(8,128)(2,1)}, u32[]{:S(2)}) %copy-start) | copy-done | bytes 4194328
  10.1 0.0 copy-start.5
  10.1 2.4 %shard_map.68 = (f32[8,8,512]{2,1,0:T(8,128)S(1)}, f32[32,1024]{1,0:T(8,128)S(1)}) custom-call(bf16[1024,2048]{1,0:T(8,128)(2,1)S(1)} %copy-done, bf16[512,768]{1,0:T(8,128)(2,1)S(1)} %copy-done.2, bf16[32,2048]{1,0:T(8,128)(2,1)S(1)} %bitcast.7, bf16[48,768]{1,0:T(8,128)(2,1)S(1)} %bitcast.8), custom_call_target="tpu_custom_call" | custom-call | flops 1000000000 | bytes 5000000 | tf_op jit(solution)/shard_map/pallas_call | solution.py:158
  12.5 13.6 %all_to_all.40.got_ref = f32[8,8,512]{2,1,0:T(8,128)S(1)} all-to-all(f32[8,8,512]{2,1,0:T(8,128)S(1)} %get-tuple-element.4), channel_id=1, replica_groups=mesh['dp'=64,'tensor'=8] {'tensor'}, dimensions={0} | all-to-all | bytes 262144 | tf_op jit(solution)/shard_map/all_to_all | solution.py:161
  26.1 0.7 broadcast_in_dim.12
  26.8 4.4 %all-to-all-start.4 = ((f32[8,8,512]{2,1,0:T(8,128)}), f32[8,8,512]{2,1,0:T(8,128)S(1)}, u32[]{:S(2)}, u32[]{:S(2)}) async-start(f32[8,8,512]{2,1,0:T(8,128)} %broadcast_in_dim.12), calls=%async_computation.4 | async-start | bytes 262144 | tf_op jit(solution)/shard_map/all_to_all | solution.py:168
  31.2 5.7 %all-to-all-done.4.everyone_ref = f32[8,8,512]{2,1,0:T(8,128)S(1)} async-done(((f32[8,8,512]{2,1,0:T(8,128)}), f32[8,8,512]{2,1,0:T(8,128)S(1)}, u32[]{:S(2)}, u32[]{:S(2)}) %all-to-all-start.4) | async-done | bytes 131104 | tf_op jit(solution)/shard_map/all_to_all | solution.py:168
  36.9 0.0 copy-done.5
  36.9 1.8 %shard_map.70 = f32[4,200,384]{2,1,0:T(8,128)} custom-call(s32[1]{0:T(128)} %bitcast.4.core_ref, f32[8,8,512]{2,1,0:T(8,128)S(1)} %all-to-all-done.4.everyone_ref, s32[2,512]{1,0:T(2,128)S(1)} %bitcast.9, bf16[512,768]{1,0:T(8,128)(2,1)S(1)} %copy-done.2), custom_call_target="tpu_custom_call" | custom-call | flops 1000000000 | bytes 3000000 | tf_op jit(solution)/shard_map/pallas_call | solution.py:169
  38.6 3.5 %all-to-all-start.5 = ((f32[4,200,384]{2,1,0:T(8,128)}), f32[4,200,384]{2,1,0:T(8,128)S(1)}, u32[]{:S(2)}, u32[]{:S(2)}) async-start(f32[4,200,384]{2,1,0:T(8,128)} %shard_map.70), calls=%async_computation.5 | async-start | bytes 2457600 | tf_op jit(solution)/shard_map/all_to_all | solution.py:44
  42.2 0.1 copy.9
  42.3 0.2 reshape.27.ids_ref
  42.5 0.0 copy-start.1
  42.5 2.2 %copy-done.1 = bf16[1024,2048]{1,0:T(8,128)(2,1)S(1)} copy-done((bf16[1024,2048]{1,0:T(8,128)(2,1)S(1)}, bf16[1024,2048]{1,0:T(8,128)(2,1)}, u32[]{:S(2)}) %copy-start.1) | copy-done | bytes 4194328
  44.7 3.3 %shard_map.69 = f32[64,32,256]{2,1,0:T(8,128)} custom-call(s32[64]{0:T(128)S(1)} %broadcast_select_fusion.place_ref, f32[8,8,512]{2,1,0:T(8,128)S(1)} %all_to_all.40.got_ref, f32[32,1024]{1,0:T(8,128)S(1)} %get-tuple-element.5.hproj_ref, s32[1,1024]{1,0:T(1,128)S(1)} %reshape.27.ids_ref, bf16[1024,2048]{1,0:T(8,128)(2,1)S(1)} %copy-done.1), custom_call_target="tpu_custom_call" | custom-call | flops 1000000000 | bytes 6000000 | tf_op jit(solution)/shard_map/pallas_call | solution.py:162
  48.0 6.0 %all-to-all-done.5 = f32[4,200,384]{2,1,0:T(8,128)S(1)} async-done(((f32[4,200,384]{2,1,0:T(8,128)}), f32[4,200,384]{2,1,0:T(8,128)S(1)}, u32[]{:S(2)}, u32[]{:S(2)}) %all-to-all-start.5) | async-done | bytes 1228832 | tf_op jit(solution)/shard_map/all_to_all | solution.py:44
  54.0 3.6 %all-to-all-start.1 = ((f32[4,16,32,256]{3,2,1,0:T(8,128)}), f32[4,16,32,256]{3,2,1,0:T(8,128)S(1)}, u32[]{:S(2)}, u32[]{:S(2)}) async-start(f32[4,16,32,256]{3,2,1,0:T(8,128)} %bitcast.2), calls=%async_computation.1 | async-start | bytes 4194304 | tf_op jit(solution)/shard_map/all_to_all | solution.py:44
  57.6 0.8 reduce_sum.48
  58.4 0.7 slice.17
  59.1 1.0 slice.16
  60.1 0.7 pad_maximum_fusion
  60.8 13.2 %all-to-all-done.1 = f32[4,16,32,256]{3,2,1,0:T(8,128)S(1)} async-done(((f32[4,16,32,256]{3,2,1,0:T(8,128)}), f32[4,16,32,256]{3,2,1,0:T(8,128)S(1)}, u32[]{:S(2)}, u32[]{:S(2)}) %all-to-all-start.1) | async-done | bytes 2097184 | tf_op jit(solution)/shard_map/all_to_all | solution.py:44
  74.1 3.5 %all-to-all-start.6 = ((f32[4,56,384]{2,1,0:T(8,128)}), f32[4,56,384]{2,1,0:T(8,128)S(1)}, u32[]{:S(2)}, u32[]{:S(2)}) async-start(f32[4,56,384]{2,1,0:T(8,128)} %pad_maximum_fusion), calls=%async_computation.6 | async-start | bytes 688128 | tf_op jit(solution)/shard_map/all_to_all | solution.py:44
  77.5 1.0 reduce_sum.45
  78.5 6.1 %all-to-all-done.6 = f32[4,56,384]{2,1,0:T(8,128)S(1)} async-done(((f32[4,56,384]{2,1,0:T(8,128)}), f32[4,56,384]{2,1,0:T(8,128)S(1)}, u32[]{:S(2)}, u32[]{:S(2)}) %all-to-all-start.6) | async-done | bytes 344096 | tf_op jit(solution)/shard_map/all_to_all | solution.py:44
  84.6 3.5 %all-to-all-start.2 = ((f32[4,4,32,256]{3,2,1,0:T(8,128)}), f32[4,4,32,256]{3,2,1,0:T(8,128)S(1)}, u32[]{:S(2)}, u32[]{:S(2)}) async-start(f32[4,4,32,256]{3,2,1,0:T(8,128)} %bitcast.3), calls=%async_computation.2 | async-start | bytes 1048576 | tf_op jit(solution)/shard_map/all_to_all | solution.py:44
  88.2 0.7 pad_maximum_fusion.1
  88.8 7.3 %all-to-all-done.2 = f32[4,4,32,256]{3,2,1,0:T(8,128)S(1)} async-done(((f32[4,4,32,256]{3,2,1,0:T(8,128)}), f32[4,4,32,256]{3,2,1,0:T(8,128)S(1)}, u32[]{:S(2)}, u32[]{:S(2)}) %all-to-all-start.2) | async-done | bytes 524320 | tf_op jit(solution)/shard_map/all_to_all | solution.py:44
  96.1 12.2 %all-to-all-start.7 = ((f32[4,16,384]{2,1,0:T(8,128)}), f32[4,16,384]{2,1,0:T(8,128)S(1)}, u32[]{:S(2)}, u32[]{:S(2)}) async-start(f32[4,16,384]{2,1,0:T(8,128)} %pad_maximum_fusion.1), calls=%async_computation.7 | async-start | bytes 196608 | tf_op jit(solution)/shard_map/all_to_all | solution.py:44
  108.3 13.0 %all-to-all-done.7.input_ref = f32[4,16,384]{2,1,0:T(8,128)S(1)} async-done(((f32[4,16,384]{2,1,0:T(8,128)}), f32[4,16,384]{2,1,0:T(8,128)S(1)}, u32[]{:S(2)}, u32[]{:S(2)}) %all-to-all-start.7) | async-done | bytes 98336 | tf_op jit(solution)/shard_map/all_to_all | solution.py:44
  121.3 17.4 %all_to_all.41.hidden_ref = f32[4,32,256]{2,1,0:T(8,128)S(1)} all-to-all(f32[4,32,256]{2,1,0:T(8,128)S(1)} %reduce_sum.46), channel_id=1, replica_groups={{0,32,64,96},{1,33,65,97},{2,34,66,98},{3,35,67,99},{4,36,68,100},{5,37..., dimensions={0} | all-to-all | bytes 262144 | tf_op jit(solution)/shard_map/all_to_all | solution.py:44
  138.7 0.6 shard_map.71
  (9 shorter events, 0.1 us)
Async XLA Ops:
  0.6 7.3 %copy-start.2 = (bf16[512,768]{1,0:T(8,128)(2,1)S(1)}, bf16[512,768]{1,0:T(8,128)(2,1)}, u32[]{:S(2)}) copy-start(bf16[512,768]{1,0:T(8,128)(2,1)} %inputs_ref.3) | copy-start | bytes 2359300
  0.6 7.3 %copy-start.3 = (bf16[2048,32]{0,1:T(8,128)(2,1)S(1)}, bf16[2048,32]{0,1:T(8,128)(2,1)}, u32[]{:S(2)}) copy-start(bf16[2048,32]{0,1:T(8,128)(2,1)} %param.9) | copy-start | bytes 393220
  0.7 7.3 %copy-start.4 = (bf16[768,48]{0,1:T(8,128)(2,1)S(1)}, bf16[768,48]{0,1:T(8,128)(2,1)}, u32[]{:S(2)}) copy-start(bf16[768,48]{0,1:T(8,128)(2,1)} %param.8) | copy-start | bytes 221188
  7.9 2.2 %copy-start = (bf16[1024,2048]{1,0:T(8,128)(2,1)S(1)}, bf16[1024,2048]{1,0:T(8,128)(2,1)}, u32[]{:S(2)}) copy-start(bf16[1024,2048]{1,0:T(8,128)(2,1)} %reshape.26.grads_ref) | copy-start | bytes 12582916
  10.1 26.7 %copy-start.5 = (s32[512,2]{0,1:T(2,128)S(1)}, s32[512,2]{0,1:T(2,128)}, u32[]{:S(2)}) copy-start(s32[512,2]{0,1:T(2,128)} %param.6) | copy-start | bytes 12292
  26.8 10.1 %all-to-all-start.4 = ((f32[8,8,512]{2,1,0:T(8,128)}), f32[8,8,512]{2,1,0:T(8,128)S(1)}, u32[]{:S(2)}, u32[]{:S(2)}) async-start(f32[8,8,512]{2,1,0:T(8,128)} %broadcast_in_dim.12), calls=%async_computation.4 | async-start | bytes 262144 | tf_op jit(solution)/shard_map/all_to_all | solution.py:168
  38.6 15.4 %all-to-all-start.5 = ((f32[4,200,384]{2,1,0:T(8,128)}), f32[4,200,384]{2,1,0:T(8,128)S(1)}, u32[]{:S(2)}, u32[]{:S(2)}) async-start(f32[4,200,384]{2,1,0:T(8,128)} %shard_map.70), calls=%async_computation.5 | async-start | bytes 2457600 | tf_op jit(solution)/shard_map/all_to_all | solution.py:44
  42.5 2.2 %copy-start.1 = (bf16[1024,2048]{1,0:T(8,128)(2,1)S(1)}, bf16[1024,2048]{1,0:T(8,128)(2,1)}, u32[]{:S(2)}) copy-start(bf16[1024,2048]{1,0:T(8,128)(2,1)} %reshape.26.grads_ref) | copy-start | bytes 12582916
  54.0 20.1 %all-to-all-start.1 = ((f32[4,16,32,256]{3,2,1,0:T(8,128)}), f32[4,16,32,256]{3,2,1,0:T(8,128)S(1)}, u32[]{:S(2)}, u32[]{:S(2)}) async-start(f32[4,16,32,256]{3,2,1,0:T(8,128)} %bitcast.2), calls=%async_computation.1 | async-start | bytes 4194304 | tf_op jit(solution)/shard_map/all_to_all | solution.py:44
  74.1 10.5 %all-to-all-start.6 = ((f32[4,56,384]{2,1,0:T(8,128)}), f32[4,56,384]{2,1,0:T(8,128)S(1)}, u32[]{:S(2)}, u32[]{:S(2)}) async-start(f32[4,56,384]{2,1,0:T(8,128)} %pad_maximum_fusion), calls=%async_computation.6 | async-start | bytes 688128 | tf_op jit(solution)/shard_map/all_to_all | solution.py:44
  84.6 11.5 %all-to-all-start.2 = ((f32[4,4,32,256]{3,2,1,0:T(8,128)}), f32[4,4,32,256]{3,2,1,0:T(8,128)S(1)}, u32[]{:S(2)}, u32[]{:S(2)}) async-start(f32[4,4,32,256]{3,2,1,0:T(8,128)} %bitcast.3), calls=%async_computation.2 | async-start | bytes 1048576 | tf_op jit(solution)/shard_map/all_to_all | solution.py:44
  96.1 25.2 %all-to-all-start.7 = ((f32[4,16,384]{2,1,0:T(8,128)}), f32[4,16,384]{2,1,0:T(8,128)S(1)}, u32[]{:S(2)}, u32[]{:S(2)}) async-start(f32[4,16,384]{2,1,0:T(8,128)} %pad_maximum_fusion.1), calls=%async_computation.7 | async-start | bytes 196608 | tf_op jit(solution)/shard_map/all_to_all | solution.py:44

commit v3 on v2

v3 whole, which is shorter than its diff:
```python
import jax
import jax.numpy as jnp
from jax import lax
from jax.experimental import pallas as pl
from jax.experimental.pallas import tpu as pltpu
from jax.sharding import PartitionSpec as P

FF = 16384
EXPERTS = 8
PROBES = 48
HPROBES = 32
EPS = 1e-06
AXES = ("dp", "tensor")
PARAMS = pltpu.CompilerParams(vmem_limit_bytes=40 * 1024 * 1024)
VMEM = pl.BlockSpec(memory_space=pltpu.VMEM)
SMEM = pl.BlockSpec(memory_space=pltpu.SMEM)


def linear(x, zh, y, t):
    return ((x * 4 + zh) * 4 + y) * 8 + t


def ring_groups(first):
    groups = []
    for zh in range(4):
        for t in range(8):
            along_x = (t % 2 == 0) == first
            for other in range(4):
                groups.append(
                    [linear(i, zh, other, t) if along_x else linear(other, zh, i, t) for i in range(4)]
                )
    return groups


def zh_groups():
    return [
        [linear(x, zh, y, t) for zh in range(4)] for x in range(4) for y in range(4) for t in range(8)
    ]


def swap(block, groups):
    return lax.all_to_all(block, AXES, 0, 0, axis_index_groups=groups)


def nt(left, right, **kw):
    return lax.dot_general(
        left, right, (((1,), (1,)), ((), ())), preferred_element_type=jnp.float32, **kw
    )


def projection_kernel(inputs_ref, probes_ref, send_ref):
    proj = nt(probes_ref[...], inputs_ref[...])
    for t in range(8):
        send_ref[t, 0:6] = proj[6 * t : 6 * t + 6]
        send_ref[t, 6:8] = jnp.zeros_like(send_ref[t, 6:8])


def order_matrix():
    row = lax.broadcasted_iota(jnp.int32, (256, 256), 0)
    column = lax.broadcasted_iota(jnp.int32, (256, 256), 1)
    source = ((row >> 1) & 7) * 32 + (row >> 4) * 2 + (row & 1)
    return jnp.where(column == source, 1.0, 0.0).astype(jnp.bfloat16)


def grads_kernel(view_ref, hprobes_ref, rows_ref, hproj_ref, squares_ref, part_ref):
    order = order_matrix()

    def step(i, carry):
        for half in range(2):
            first = i * 4 + half * 2
            pair = jnp.concatenate(
                [view_ref[pl.ds((first + m) * 8, 8)].reshape(256, 128) for m in range(2)], axis=1
            )
            ordered = jnp.dot(order, pair, preferred_element_type=jnp.float32)
            for m in range(2):
                at = pl.multiple_of((first + m) * 16, 16)
                part = jnp.zeros((16, 128), jnp.float32)
                for tile in range(16):
                    piece = ordered[16 * tile : 16 * tile + 16, 128 * m : 128 * (m + 1)]
                    part = part + piece * piece
                    rows_ref[pl.ds(at, 16), 128 * tile : 128 * (tile + 1)] = piece.astype(jnp.bfloat16)
                part_ref[pl.ds(at, 16)] = part
        return carry

    lax.fori_loop(0, 16, step, 0)
    squares = nt(jnp.ones((8, 128), jnp.float32), part_ref[...], precision=lax.Precision.HIGHEST)
    squares_ref[0:1] = squares[0:1, 0:512]
    squares_ref[1:2] = squares[0:1, 512:1024]
    hproj_ref[...] = nt(hprobes_ref[...], rows_ref[...])


def between_kernel(got_ref, squares_ref, send_ref):
    mine = jnp.sum(got_ref[...], axis=0)
    for t in range(8):
        send_ref[t, 0:6] = mine[0:6]
        send_ref[t, 6:8] = squares_ref[...]


def hidden_kernel(place_ref, got_ref, hproj_ref, ids_ref, rows_ref, out_ref):
    got = jnp.sum(got_ref[...], axis=0)
    squares = jnp.concatenate([got[6:7], got[7:8]], axis=1)
    scaled = hproj_ref[...] * jnp.minimum(1.0, FF / (squares + EPS))
    ids = ids_ref[...]
    weights = jnp.concatenate(
        [jnp.where(ids == e, scaled, 0.0).astype(jnp.bfloat16) for e in range(EXPERTS)], axis=0
    )
    rows = rows_ref[...]
    for b in range(8):
        product = jnp.dot(
            weights, rows[:, 256 * b : 256 * (b + 1)], preferred_element_type=jnp.float32
        ).T
        for c in range(8):
            place = place_ref[8 * b + c]
            out_ref[place, 0:32] = product[32 * c : 32 * c + 32, 0:128]
            out_ref[place, 32:64] = product[32 * c : 32 * c + 32, 128:256]


def input_kernel(place_ref, everyone_ref, ids_ref, inputs_ref, partly_ref, out_ref):
    del partly_ref
    projected = jnp.concatenate([everyone_ref[t, 0:6] for t in range(8)], axis=0)
    ids = ids_ref[...]
    routed = [(ids[0:1] == e) | (ids[1:2] == e) for e in range(EXPERTS)]
    weights = jnp.concatenate(
        [jnp.where(r, projected, 0.0).astype(jnp.bfloat16) for r in routed], axis=0
    )
    product = jnp.dot(weights, inputs_ref[...], preferred_element_type=jnp.float32).T
    lane = lax.broadcasted_iota(jnp.int32, (4, 128), 1)
    counts = jnp.zeros((4, 128), jnp.float32)
    for e in range(EXPERTS):
        total = jnp.sum(jnp.where(routed[e], 1.0, 0.0), axis=1, keepdims=True)
        counts = jnp.where(lane == e, total, counts)
    for d in range(64):
        place = place_ref[d]
        for m in range(3):
            out_ref[place, 64 + 12 * m : 76 + 12 * m] = product[
                12 * d : 12 * d + 12, 128 * m : 128 * (m + 1)
            ]
        out_ref[place, 100:104] = counts


def last_kernel(block_ref, input_out, hidden_out):
    total = jnp.sum(block_ref[...], axis=0)
    for out, first, rows, tiles, repeat in (
        (input_out, 64, 12, 3, PROBES),
        (hidden_out, 0, 32, 2, HPROBES),
    ):
        for m in range(tiles):
            owner = (lax.broadcasted_iota(jnp.int32, (1, 128), 1) + 128 * m) // repeat
            counts = jnp.zeros((1, 128), jnp.float32)
            for e in range(EXPERTS):
                counts = jnp.where(owner == e, total[100:101, e : e + 1], counts)
            out[:, 128 * m : 128 * (m + 1)] = total[first + rows * m : first + rows * (m + 1)] / counts


def call(kernel, out_shape, in_specs, out_specs, flops, size, **kw):
    return pl.pallas_call(
        kernel,
        out_shape=out_shape,
        in_specs=in_specs,
        out_specs=out_specs,
        compiler_params=PARAMS,
        cost_estimate=pl.CostEstimate(flops=flops, bytes_accessed=size, transcendentals=0),
        **kw,
    )


def shape(*dims):
    return jax.ShapeDtypeStruct(dims, jnp.float32)


def body(inputs, expert_ids, hidden_grads, input_probes, hidden_probes):
    tokens = inputs.shape[0]
    core = lax.axis_index("tensor") % 2
    dp = jnp.arange(64, dtype=jnp.int32)
    x, zh, y = dp // 16, dp // 4 % 4, dp % 4
    place = jnp.where(core == 0, (x * 4 + y) * 4 + zh, (y * 4 + x) * 4 + zh)
    ids_pair = expert_ids.T
    ids_row = expert_ids.reshape(1, 2 * tokens)

    send = call(projection_kernel, shape(8, 8, tokens), [VMEM] * 2, VMEM, 10**8, 10**6)(
        inputs, input_probes.T
    )
    got = lax.all_to_all(send, "tensor", 0, 0)
    view = hidden_grads.reshape(tokens, 2, 16, 128).transpose(0, 2, 1, 3).reshape(tokens, 32, 128)
    rows, hproj, squares = call(
        grads_kernel,
        (
            jax.ShapeDtypeStruct((2 * tokens, 2048), jnp.bfloat16),
            shape(HPROBES, 2 * tokens),
            shape(2, tokens),
        ),
        [VMEM] * 2,
        (VMEM,) * 3,
        4 * 10**9,
        9 * 10**6,
        scratch_shapes=[pltpu.VMEM((2 * tokens, 128), jnp.float32)],
    )(view, hidden_probes.T)
    send = call(between_kernel, shape(8, 8, tokens), [VMEM] * 2, VMEM, 10**5, 10**5)(got, squares)
    everyone = lax.all_to_all(send, "tensor", 0, 0)
    block = call(
        hidden_kernel, shape(64, 104, 128), [SMEM] + [VMEM] * 4, VMEM, 10**9, 6 * 10**6
    )(place, everyone, hproj, ids_row, rows)
    block = call(
        input_kernel,
        shape(64, 104, 128),
        [SMEM] + [VMEM] * 4,
        VMEM,
        10**9,
        3 * 10**6,
        input_output_aliases={4: 0},
    )(place, everyone, ids_pair, inputs, block)
    block = jnp.sum(swap(block.reshape(4, 16, 104, 128), ring_groups(True)), axis=0)
    block = jnp.sum(swap(block.reshape(4, 4, 104, 128), ring_groups(False)), axis=0)
    block = swap(block, zh_groups())
    return call(
        last_kernel, (shape(12, 384), shape(32, 256)), [VMEM], (VMEM, VMEM), 10**5, 10**5
    )(block)


def solution(mesh):
    return jax.shard_map(
        body,
        mesh=mesh,
        in_specs=(
            P("dp", "tensor"),
            P("dp", None),
            P("dp", None, "tensor"),
            P("tensor", None),
            P("tensor", None),
        ),
        out_specs=(P(("tensor", "dp"), None), P(("tensor", "dp"), None)),
        check_vma=False,
    )
```

time: 140 us -> 111 us (0.79)
  waiting for transfers between devices: 51.3 us -> 5.32 us
  blocking collectives: 30.9 us -> 68.4 us
  starting transfers between devices: 30.6 us -> 13.9 us
  local copies, waits for them, and re-layouts: 14.3 us -> 9.57 us
  Pallas kernels: 8.07 us -> 11.6 us
  other arithmetic: 3.26 us -> 1.25 us
    all_to_all x1 -> x3, blocking collectives: 17.4 us -> 68.4 us  [swap(): return lax.all_to_all(block, AXES, 0, 0, axis_index_groups=groups)]
    all_to_all x6 -> x2, waiting for transfers between devices: 51.3 us -> 5.32 us  [the longest x1 5.32 us: body(): everyone = lax.all_to_all(send, 'tensor', 0, 0)]
    all_to_all x6 -> x2, starting transfers between devices: 30.6 us -> 13.9 us  [the longest x1 8.76 us: body(): got = lax.all_to_all(send, 'tensor', 0, 0)]
    all_to_all x1 -> x0, blocking collectives: 13.6 us -> none  [body(): got = lax.all_to_all(send, 'tensor', 0, 0)]
    reshape x2 -> x0, local copies, waits for them, and re-layouts: 7.27 us -> none  [the longest x1 7.26 us: body(): hidden_grads = hidden_grads.reshape(2 * tokens, -1)]
    unnamed x13 -> x17, local copies, waits for them, and re-layouts: 4.52 us -> 9.39 us
    pallas_call x4 -> x6, Pallas kernels: 8.07 us -> 11.6 us  [the longest x1 6.01 us: body(): call(grads_kernel, (jax.ShapeDtypeStruct((2 * tokens, 2048), jnp.bfloat16...]
    slice x4 -> x0, local copies, waits for them, and re-layouts: 1.7 us -> none  [the longest x1 0.98 us: body(): inp[:192].reshape(4, 48, 384)]
  transfers between devices with their start and end apart: 6 -> 2, of which waited for: 6 -> 1; matrix products, arithmetic and copies ran while one was open for 4% -> 0% of each run, Pallas kernels for 2% -> 5%
where the time goes in v3:
time: 111 us
  blocking collectives  68.4 us (62%)
  starting transfers between devices  13.9 us (13%)
  Pallas kernels  11.6 us (10%)
  local copies, waits for them, and re-layouts  9.57 us (9%)
  waiting for transfers between devices  5.32 us (5%)
  other arithmetic  1.25 us (1%)
    all_to_all x3, blocking collectives, swap(): return lax.all_to_all(block, AXES, 0, 0, axis_index_groups=groups)  68.4 us
    unnamed x17, local copies, waits for them, and re-layouts  9.39 us
    all_to_all x1, starting transfers between devices, body(): got = lax.all_to_all(send, 'tensor', 0, 0)  8.76 us
    pallas_call x1, Pallas kernels, body(): call(grads_kernel, (jax.ShapeDtypeStruct((2 * tokens, 2048), jnp.bfloat16...  6.01 us
    all_to_all x1, waiting for transfers between devices, body(): everyone = lax.all_to_all(send, 'tensor', 0, 0)  5.32 us
    all_to_all x1, starting transfers between devices, body(): everyone = lax.all_to_all(send, 'tensor', 0, 0)  5.12 us
  transfers between devices with their start and end apart: 2, of which 1 were waited for; matrix products, arithmetic and copies ran while one was open for 0% of the time, Pallas kernels for 5%

profile of v3, /device:TPU:32, one launch (start us, length us, event | category | flops | bytes accessed | tf_op | source)
XLA Modules:
  0.0 110.7 jit_solution(17370444380532384922)
XLA Ops:
  0.6 0.0 copy-start.2
  0.6 1.1 %copy-done.2 = bf16[512,768]{1,0:T(8,128)(2,1)S(1)} copy-done((bf16[512,768]{1,0:T(8,128)(2,1)S(1)}, bf16[512,768]{1,0:T(8,128)(2,1)}, u32[]{:S(2)}) %copy-start.2) | copy-done | bytes 786456
  1.8 0.0 copy-start.4
  1.8 0.9 copy-done.4
  2.7 1.0 shard_map.68
  3.6 8.8 %all-to-all-start = ((f32[8,8,512]{2,1,0:T(8,128)}), f32[8,8,512]{2,1,0:T(8,128)S(1)}, u32[]{:S(2)}, u32[]{:S(2)}) async-start(f32[8,8,512]{2,1,0:T(8,128)} %shard_map.68), calls=%async_computation | async-start | bytes 262144 | tf_op jit(solution)/shard_map/all_to_all | solution.py:183
  12.4 0.0 copy-start.6
  12.4 2.2 %copy-done.6 = bf16[512,2,2048]{2,1,0:T(2,128)(2,1)S(1)} copy-done((bf16[512,2,2048]{2,1,0:T(2,128)(2,1)S(1)}, bf16[512,2,2048]{2,1,0:T(2,128)(2,1)}, u32[]{:S(2)}) %copy-start.6) | copy-done | bytes 4194328
  14.6 0.0 copy-start.7
  14.6 0.9 copy-done.7
  15.5 0.0 copy-start.5
  15.5 6.0 %shard_map.69 = (bf16[1024,2048]{1,0:T(8,128)(2,1)S(1)}, f32[32,1024]{1,0:T(8,128)S(1)}, f32[2,512]{1,0:T(2,128)S(1)}) custom-call(bf16[512,32,128]{2,1,0:T(8,128)(2,1)S(1)} %bitcast.13, bf16[32,2048]{1,0:T(8,128)(2,1)S(1)} %bitcast.14), custom_call_target="tpu_custom_call" | custom-call | flops 4000000000 | bytes 9000000 | tf_op jit(solution)/shard_map/pallas_call | solution.py:185
  21.5 0.0 copy-start
  21.5 1.9 %copy-done = bf16[1024,2048]{1,0:T(8,128)(2,1)} copy-done((bf16[1024,2048]{1,0:T(8,128)(2,1)}, bf16[1024,2048]{1,0:T(8,128)(2,1)S(1)}, u32[]{:S(2)}) %copy-start) | copy-done | bytes 4194328
  23.5 0.0 all-to-all-done.got_ref
  23.5 0.7 shard_map.70
  24.1 5.1 %all-to-all-start.1 = ((f32[8,8,512]{2,1,0:T(8,128)}), f32[8,8,512]{2,1,0:T(8,128)S(1)}, u32[]{:S(2)}, u32[]{:S(2)}) async-start(f32[8,8,512]{2,1,0:T(8,128)} %shard_map.70), calls=%async_computation.1 | async-start | bytes 262144 | tf_op jit(solution)/shard_map/all_to_all | solution.py:199
  29.3 0.0 copy-done.5
  29.3 0.1 copy.13
  29.4 0.2 reshape.21.ids_ref
  29.6 5.3 %all-to-all-done.1.got_ref.everyone_ref = f32[8,8,512]{2,1,0:T(8,128)S(1)} async-done(((f32[8,8,512]{2,1,0:T(8,128)}), f32[8,8,512]{2,1,0:T(8,128)S(1)}, u32[]{:S(2)}, u32[]{:S(2)}) %all-to-all-start.1) | async-done | bytes 131104 | tf_op jit(solution)/shard_map/all_to_all | solution.py:199
  34.9 0.0 copy-start.1
  34.9 2.2 %copy-done.1 = bf16[1024,2048]{1,0:T(8,128)(2,1)S(1)} copy-done((bf16[1024,2048]{1,0:T(8,128)(2,1)S(1)}, bf16[1024,2048]{1,0:T(8,128)(2,1)}, u32[]{:S(2)}) %copy-start.1) | copy-done | bytes 4194328
  37.1 0.0 copy-start.3
  37.1 2.0 %shard_map.71.partly_ref = f32[64,104,128]{2,1,0:T(8,128)S(1)} custom-call(s32[64]{0:T(128)S(1)} %broadcast_select_fusion.place_ref, f32[8,8,512]{2,1,0:T(8,128)S(1)} %all-to-all-done.1.got_ref.everyone_ref, f32[32,1024]{1,0:T(8,128)S(1)} %get-tuple-element.6.hproj_ref, s32[1,1024]{1,0:T(1,128)S(1)} %reshape.21.ids_ref, bf16[1024,2048]{1,0:T(8,128)(2,1)S(1)} %copy-done.1), custom_call_target="tpu_custom_call" | custom-call | flops 1000000000 | bytes 6000000 | tf_op jit(solution)/shard_map/pallas_call | solution.py:200
  39.1 0.0 copy-done.3
  39.1 1.2 %shard_map.72 = f32[64,104,128]{2,1,0:T(8,128)S(1)} custom-call(s32[64]{0:T(128)S(1)} %broadcast_select_fusion.place_ref, f32[8,8,512]{2,1,0:T(8,128)S(1)} %all-to-all-done.1.got_ref.everyone_ref, s32[2,512]{1,0:T(2,128)S(1)} %bitcast.12, bf16[512,768]{1,0:T(8,128)(2,1)S(1)} %copy-done.3, ...), custom_call_target="tpu_custom_call", output_to_operand_aliasing={{}: (4, {})} | custom-call | flops 1000000000 | bytes 3000000 | tf_op jit(solution)/shard_map/pallas_call | solution.py:203
  40.3 26.1 %all_to_all.25 = f32[4,16,104,128]{3,2,1,0:T(8,128)S(1)} all-to-all(f32[4,16,104,128]{3,2,1,0:T(8,128)S(1)} %bitcast.10), channel_id=1, replica_groups={{0,128,256,384},{8,136,264,392},{16,144,272,400},{24,152,280,408},{1,9,..., dimensions={0} | all-to-all | bytes 6815744 | tf_op jit(solution)/shard_map/all_to_all | solution.py:42
  66.4 1.2 %reduce_sum.18 = f32[16,104,128]{2,1,0:T(8,128)} reduce(f32[4,16,104,128]{3,2,1,0:T(8,128)S(1)} %all_to_all.25, f32[]{:T(128)} %constant.65.clone.1), dimensions={0}, to_apply=%region_0.1 | reduce | flops 638976 | bytes 4259844 | tf_op jit(solution)/shard_map/reduce_sum | solution.py:212
  67.6 13.3 %all_to_all.26 = f32[4,4,104,128]{3,2,1,0:T(8,128)S(1)} all-to-all(f32[4,4,104,128]{3,2,1,0:T(8,128)} %bitcast.15), channel_id=1, replica_groups={{0,8,16,24},{128,136,144,152},{256,264,272,280},{384,392,400,408},{1,12..., dimensions={0} | all-to-all | bytes 1703936 | tf_op jit(solution)/shard_map/all_to_all | solution.py:42
  80.9 29.0 %all_to_all.27.block_ref = f32[4,104,128]{2,1,0:T(8,128)S(1)} all-to-all(f32[4,104,128]{2,1,0:T(8,128)S(1)} %reduce_sum.19), channel_id=1, replica_groups={{0,32,64,96},{1,33,65,97},{2,34,66,98},{3,35,67,99},{4,36,68,100},{5,37..., dimensions={0} | all-to-all | bytes 425984 | tf_op jit(solution)/shard_map/all_to_all | solution.py:42
  109.9 0.7 shard_map.73
  (2 shorter events, 0.1 us)
Async XLA Ops:
  0.6 1.1 %copy-start.2 = (bf16[512,768]{1,0:T(8,128)(2,1)S(1)}, bf16[512,768]{1,0:T(8,128)(2,1)}, u32[]{:S(2)}) copy-start(bf16[512,768]{1,0:T(8,128)(2,1)} %inputs_ref.3) | copy-start | bytes 2359300
  1.8 0.9 copy-start.4
  3.6 19.8 %all-to-all-start = ((f32[8,8,512]{2,1,0:T(8,128)}), f32[8,8,512]{2,1,0:T(8,128)S(1)}, u32[]{:S(2)}, u32[]{:S(2)}) async-start(f32[8,8,512]{2,1,0:T(8,128)} %shard_map.68), calls=%async_computation | async-start | bytes 262144 | tf_op jit(solution)/shard_map/all_to_all | solution.py:183
  12.4 2.2 %copy-start.6 = (bf16[512,2,2048]{2,1,0:T(2,128)(2,1)S(1)}, bf16[512,2,2048]{2,1,0:T(2,128)(2,1)}, u32[]{:S(2)}) copy-start(bf16[512,2,2048]{2,1,0:T(2,128)(2,1)} %param.7) | copy-start | bytes 12582916
  14.6 0.9 copy-start.7
  15.5 13.8 %copy-start.5 = (s32[512,2]{0,1:T(2,128)S(1)}, s32[512,2]{0,1:T(2,128)}, u32[]{:S(2)}) copy-start(s32[512,2]{0,1:T(2,128)} %param.6) | copy-start | bytes 12292
  21.5 2.0 %copy-start = (bf16[1024,2048]{1,0:T(8,128)(2,1)}, bf16[1024,2048]{1,0:T(8,128)(2,1)S(1)}, u32[]{:S(2)}) copy-start(bf16[1024,2048]{1,0:T(8,128)(2,1)S(1)} %get-tuple-element.7.rows_ref) | copy-start | bytes 12582916
  24.1 10.8 %all-to-all-start.1 = ((f32[8,8,512]{2,1,0:T(8,128)}), f32[8,8,512]{2,1,0:T(8,128)S(1)}, u32[]{:S(2)}, u32[]{:S(2)}) async-start(f32[8,8,512]{2,1,0:T(8,128)} %shard_map.70), calls=%async_computation.1 | async-start | bytes 262144 | tf_op jit(solution)/shard_map/all_to_all | solution.py:199
  34.9 2.2 %copy-start.1 = (bf16[1024,2048]{1,0:T(8,128)(2,1)S(1)}, bf16[1024,2048]{1,0:T(8,128)(2,1)}, u32[]{:S(2)}) copy-start(bf16[1024,2048]{1,0:T(8,128)(2,1)} %copy-done) | copy-start | bytes 12582916
  37.1 2.0 %copy-start.3 = (bf16[512,768]{1,0:T(8,128)(2,1)S(1)}, bf16[512,768]{1,0:T(8,128)(2,1)}, u32[]{:S(2)}) copy-start(bf16[512,768]{1,0:T(8,128)(2,1)} %inputs_ref.3) | copy-start | bytes 2359300

commit v4 on v3

--- a/solution.py
+++ b/solution.py
@@ -11,9 +11,11 @@
 HPROBES = 32
 EPS = 1e-06
 AXES = ("dp", "tensor")
-PARAMS = pltpu.CompilerParams(vmem_limit_bytes=40 * 1024 * 1024)
+LIMIT = 40 * 10**6
 VMEM = pl.BlockSpec(memory_space=pltpu.VMEM)
 SMEM = pl.BlockSpec(memory_space=pltpu.SMEM)
+HBM = pl.BlockSpec(memory_space=pltpu.HBM)
+DMA = pltpu.SemaphoreType.DMA
 
 
 def linear(x, zh, y, t):
@@ -48,11 +50,59 @@
     )
 
 
-def projection_kernel(inputs_ref, probes_ref, send_ref):
+def pick_matrix():
+    row = lax.broadcasted_iota(jnp.int32, (256, 64), 0)
+    column = lax.broadcasted_iota(jnp.int32, (256, 64), 1)
+    same = ((row >> 3) == (column >> 1)) & ((row & 1) == (column & 1))
+    return jnp.where(same, 1.0, 0.0).astype(jnp.bfloat16)
+
+
+def thirds(value):
+    high = value.astype(jnp.bfloat16).astype(jnp.float32)
+    middle = (value - high).astype(jnp.bfloat16).astype(jnp.float32)
+    rest = value - high - middle
+    return jnp.concatenate([high, middle, rest, jnp.zeros_like(value)], axis=0).astype(jnp.bfloat16)
+
+
+def norm_kernel(view_hbm, inputs_hbm, probes_hbm, send_ref, view_ref, inputs_ref, probes_ref, sems):
+    loads = [
+        pltpu.make_async_copy(
+            view_hbm.at[pl.ds(128 * c, 128)], view_ref.at[pl.ds(128 * c, 128)], sems.at[c]
+        )
+        for c in range(4)
+    ]
+    loads += [
+        pltpu.make_async_copy(inputs_hbm, inputs_ref, sems.at[4]),
+        pltpu.make_async_copy(probes_hbm, probes_ref, sems.at[5]),
+    ]
+    for load in loads:
+        load.start()
+    ones = jnp.ones((8, 128), jnp.bfloat16)
+    sums = []
+    for c in range(4):
+        loads[c].wait()
+        wide = view_ref[128 * c : 128 * c + 128].astype(jnp.float32)
+        wide = wide * wide
+        part = (wide[:, 0:8] + wide[:, 8:16]) + (wide[:, 16:24] + wide[:, 24:32])
+        part = part.reshape(1024, 128)
+        high = part.astype(jnp.bfloat16)
+        low = (part - high.astype(jnp.float32)).astype(jnp.bfloat16)
+        sums.append((nt(ones, high) + nt(ones, low))[0:1])
+    lanes = thirds(jnp.concatenate(sums, axis=1))
+    pick = pick_matrix()
+    picked = [
+        jnp.dot(lanes[:, 256 * b : 256 * (b + 1)], pick, preferred_element_type=jnp.float32)
+        for b in range(16)
+    ]
+    picked = jnp.sum(jnp.concatenate(picked, axis=1), axis=0, keepdims=True)
+    for t in range(8):
+        send_ref[t, 6:7] = picked[:, 0:512]
+        send_ref[t, 7:8] = picked[:, 512:1024]
+    loads[4].wait()
+    loads[5].wait()
     proj = nt(probes_ref[...], inputs_ref[...])
     for t in range(8):
         send_ref[t, 0:6] = proj[6 * t : 6 * t + 6]
-        send_ref[t, 6:8] = jnp.zeros_like(send_ref[t, 6:8])
 
 
 def order_matrix():
@@ -62,38 +112,62 @@
     return jnp.where(column == source, 1.0, 0.0).astype(jnp.bfloat16)
 
 
-def grads_kernel(view_ref, hprobes_ref, rows_ref, hproj_ref, squares_ref, part_ref):
+def grads_kernel(
+    view_hbm, hprobes_hbm, rows_hbm, hproj_ref, view_ref, rows_ref, hprobes_ref, sems, out_sems
+):
+    loads = [
+        pltpu.make_async_copy(
+            view_hbm.at[pl.ds(128 * c, 128)], view_ref.at[pl.ds(128 * c, 128)], sems.at[c]
+        )
+        for c in range(4)
+    ]
+    probe_load = pltpu.make_async_copy(hprobes_hbm, hprobes_ref, sems.at[4])
+    for load in loads:
+        load.start()
+    probe_load.start()
     order = order_matrix()
-
-    def step(i, carry):
-        for half in range(2):
-            first = i * 4 + half * 2
-            pair = jnp.concatenate(
-                [view_ref[pl.ds((first + m) * 8, 8)].reshape(256, 128) for m in range(2)], axis=1
+    stores = []
+    for c in range(4):
+        loads[c].wait()
+
+        def step(i, carry):
+            for half in range(4):
+                first = i * 8 + half * 2
+                pair = jnp.concatenate(
+                    [view_ref[pl.ds((first + m) * 8, 8)].reshape(256, 128) for m in range(2)], axis=1
+                )
+                ordered = jnp.dot(order, pair, preferred_element_type=jnp.float32)
+                for m in range(2):
+                    at = pl.multiple_of((first + m) * 16, 16)
+                    for tile in range(16):
+                        piece = ordered[16 * tile : 16 * tile + 16, 128 * m : 128 * (m + 1)]
+                        lanes = 128 * (tile % 2)
+                        rows_ref[tile // 2, pl.ds(at, 16), lanes : lanes + 128] = piece.astype(
+                            jnp.bfloat16
+                        )
+            return carry
+
+        lax.fori_loop(2 * c, 2 * c + 2, step, 0)
+        here = pl.ds(256 * c, 256)
+        store = pltpu.make_async_copy(rows_ref.at[:, here], rows_hbm.at[:, here], out_sems.at[c])
+        store.start()
+        stores.append(store)
+        if c == 0:
+            probe_load.wait()
+        total = jnp.zeros((HPROBES, 256), jnp.float32)
+        for b in range(8):
+            total = total + nt(
+                hprobes_ref[:, 256 * b : 256 * (b + 1)], rows_ref[b, 256 * c : 256 * c + 256]
             )
-            ordered = jnp.dot(order, pair, preferred_element_type=jnp.float32)
-            for m in range(2):
-                at = pl.multiple_of((first + m) * 16, 16)
-                part = jnp.zeros((16, 128), jnp.float32)
-                for tile in range(16):
-                    piece = ordered[16 * tile : 16 * tile + 16, 128 * m : 128 * (m + 1)]
-                    part = part + piece * piece
-                    rows_ref[pl.ds(at, 16), 128 * tile : 128 * (tile + 1)] = piece.astype(jnp.bfloat16)
-                part_ref[pl.ds(at, 16)] = part
-        return carry
-
-    lax.fori_loop(0, 16, step, 0)
-    squares = nt(jnp.ones((8, 128), jnp.float32), part_ref[...], precision=lax.Precision.HIGHEST)
-    squares_ref[0:1] = squares[0:1, 0:512]
-    squares_ref[1:2] = squares[0:1, 512:1024]
-    hproj_ref[...] = nt(hprobes_ref[...], rows_ref[...])
-
-
-def between_kernel(got_ref, squares_ref, send_ref):
+        hproj_ref[:, 256 * c : 256 * c + 256] = total
+    for store in stores:
+        store.wait()
+
+
+def between_kernel(got_ref, send_ref):
     mine = jnp.sum(got_ref[...], axis=0)
     for t in range(8):
-        send_ref[t, 0:6] = mine[0:6]
-        send_ref[t, 6:8] = squares_ref[...]
+        send_ref[t] = mine
 
 
 def hidden_kernel(place_ref, got_ref, hproj_ref, ids_ref, rows_ref, out_ref):
@@ -104,10 +178,9 @@
     weights = jnp.concatenate(
         [jnp.where(ids == e, scaled, 0.0).astype(jnp.bfloat16) for e in range(EXPERTS)], axis=0
     )
-    rows = rows_ref[...]
     for b in range(8):
         product = jnp.dot(
-            weights, rows[:, 256 * b : 256 * (b + 1)], preferred_element_type=jnp.float32
+            weights, rows_ref[b], preferred_element_type=jnp.float32
         ).T
         for c in range(8):
             place = place_ref[8 * b + c]
@@ -152,13 +225,13 @@
             out[:, 128 * m : 128 * (m + 1)] = total[first + rows * m : first + rows * (m + 1)] / counts
 
 
-def call(kernel, out_shape, in_specs, out_specs, flops, size, **kw):
+def call(kernel, out_shape, in_specs, out_specs, flops, size, limit=LIMIT, **kw):
     return pl.pallas_call(
         kernel,
         out_shape=out_shape,
         in_specs=in_specs,
         out_specs=out_specs,
-        compiler_params=PARAMS,
+        compiler_params=pltpu.CompilerParams(vmem_limit_bytes=limit),
         cost_estimate=pl.CostEstimate(flops=flops, bytes_accessed=size, transcendentals=0),
         **kw,
     )
@@ -174,32 +247,55 @@
     dp = jnp.arange(64, dtype=jnp.int32)
     x, zh, y = dp // 16, dp // 4 % 4, dp % 4
     place = jnp.where(core == 0, (x * 4 + y) * 4 + zh, (y * 4 + x) * 4 + zh)
+    bf16 = jnp.bfloat16
     ids_pair = expert_ids.T
     ids_row = expert_ids.reshape(1, 2 * tokens)
 
-    send = call(projection_kernel, shape(8, 8, tokens), [VMEM] * 2, VMEM, 10**8, 10**6)(
-        inputs, input_probes.T
-    )
+    bf16 = jnp.bfloat16
+    view = hidden_grads.reshape(tokens, 2, 16, 128).transpose(0, 2, 1, 3).reshape(tokens, 32, 128)
+    send = call(
+        norm_kernel,
+        shape(8, 8, tokens),
+        [HBM] * 3,
+        VMEM,
+        10**9,
+        5 * 10**6,
+        63 * 10**6,
+        scratch_shapes=[
+            pltpu.VMEM((tokens, 32, 128), bf16),
+            pltpu.VMEM((tokens, 768), bf16),
+            pltpu.VMEM((PROBES, 768), bf16),
+            DMA((6,)),
+        ],
+    )(view, inputs, input_probes.T)
     got = lax.all_to_all(send, "tensor", 0, 0)
-    view = hidden_grads.reshape(tokens, 2, 16, 128).transpose(0, 2, 1, 3).reshape(tokens, 32, 128)
-    rows, hproj, squares = call(
+    rows, hproj = call(
         grads_kernel,
-        (
-            jax.ShapeDtypeStruct((2 * tokens, 2048), jnp.bfloat16),
-            shape(HPROBES, 2 * tokens),
-            shape(2, tokens),
-        ),
-        [VMEM] * 2,
-        (VMEM,) * 3,
+        (jax.ShapeDtypeStruct((8, 2 * tokens, 256), bf16), shape(HPROBES, 2 * tokens)),
+        [HBM] * 2,
+        (HBM, VMEM),
         4 * 10**9,
         9 * 10**6,
-        scratch_shapes=[pltpu.VMEM((2 * tokens, 128), jnp.float32)],
+        55 * 10**6,
+        scratch_shapes=[
+            pltpu.VMEM((tokens, 32, 128), bf16),
+            pltpu.VMEM((8, 2 * tokens, 256), bf16),
+            pltpu.VMEM((HPROBES, 2048), bf16),
+            DMA((5,)),
+            DMA((4,)),
+        ],
     )(view, hidden_probes.T)
-    send = call(between_kernel, shape(8, 8, tokens), [VMEM] * 2, VMEM, 10**5, 10**5)(got, squares)
+    got, hproj = lax.optimization_barrier((got, hproj))
+    send = call(between_kernel, shape(8, 8, tokens), [VMEM], VMEM, 10**5, 10**5)(got)
     everyone = lax.all_to_all(send, "tensor", 0, 0)
     block = call(
-        hidden_kernel, shape(64, 104, 128), [SMEM] + [VMEM] * 4, VMEM, 10**9, 6 * 10**6
-    )(place, everyone, hproj, ids_row, rows)
+        hidden_kernel,
+        shape(64, 104, 128),
+        [SMEM] + [VMEM] * 4,
+        VMEM,
+        10**9,
+        6 * 10**6,
+    )(place, got, hproj, ids_row, rows)
     block = call(
         input_kernel,
         shape(64, 104, 128),
@@ -209,7 +305,8 @@
         3 * 10**6,
         input_output_aliases={4: 0},
     )(place, everyone, ids_pair, inputs, block)
-    block = jnp.sum(swap(block.reshape(4, 16, 104, 128), ring_groups(True)), axis=0)
+    block = swap(block.reshape(4, 16, 104, 128), ring_groups(True))
+    block = (block[0] + block[1]) + (block[2] + block[3])
     block = jnp.sum(swap(block.reshape(4, 4, 104, 128), ring_groups(False)), axis=0)
     block = swap(block, zh_groups())
     return call(

time: 111 us -> 105 us (0.946)
  waiting for transfers between devices: 5.32 us -> 0.38 us
  local copies, waits for them, and re-layouts: 9.57 us -> 5.19 us
  Pallas kernels: 11.6 us -> 15.3 us
    all_to_all x1, waiting for transfers between devices: 5.32 us -> 0.38 us  [body(): everyone = lax.all_to_all(send, 'tensor', 0, 0)]
    unnamed x17 -> x13, local copies, waits for them, and re-layouts: 9.39 us -> 5.01 us
    pallas_call x3, Pallas kernels: 7.66 us -> 11 us  [the longest x1 6.12 us: body(): call(grads_kernel, (jax.ShapeDtypeStruct((8, 2 * tokens, 256), bf16), sha...]
    reduce_sum x1 -> x0, other arithmetic: 1.19 us -> none  [body(): jnp.sum(swap(block.reshape(4, 16, 104, 128), ring_groups(True)), axis=0)]
  transfers between devices with their start and end apart: 2 -> 2, of which waited for: 1 -> 1; matrix products, arithmetic and copies ran while one was open for 0% -> 0% of each run, Pallas kernels for 5% -> 8%
where the time goes in v4:
time: 105 us; the launch traced here: 104 us
  blocking collectives  68.5 us (65%)
  Pallas kernels  15.3 us (15%)
  starting transfers between devices  13.9 us (13%)
  local copies, waits for them, and re-layouts  5.19 us (5%)
    all_to_all x3, blocking collectives, swap(): return lax.all_to_all(block, AXES, 0, 0, axis_index_groups=groups)  68.5 us
    all_to_all x1, starting transfers between devices, body(): got = lax.all_to_all(send, 'tensor', 0, 0)  8.77 us
    pallas_call x1, Pallas kernels, body(): call(grads_kernel, (jax.ShapeDtypeStruct((8, 2 * tokens, 256), bf16), sha...  6.12 us
    all_to_all x1, starting transfers between devices, body(): everyone = lax.all_to_all(send, 'tensor', 0, 0)  5.12 us
    unnamed x13, local copies, waits for them, and re-layouts  5.01 us
    pallas_call x1, Pallas kernels, body(): call(norm_kernel, shape(8, 8, tokens), [HBM] * 3, VMEM, 10 ** 9, 5 * 10 *...  4.26 us
  transfers between devices with their start and end apart: 2, of which 1 were waited for; matrix products, arithmetic and copies ran while one was open for 0% of the time, Pallas kernels for 8%

profile of v4, /device:TPU:32, one launch (start us, length us, event | category | flops | bytes accessed | tf_op | source)
XLA Modules:
  0.0 104.2 jit_solution(16451596964603138433)
XLA Ops:
  0.6 0.0 copy-start.5
  0.6 4.3 %shard_map.68 = f32[8,8,512]{2,1,0:T(8,128)} custom-call(bf16[512,32,128]{2,1,0:T(8,128)(2,1)} %bitcast.13, bf16[512,768]{1,0:T(8,128)(2,1)} %inputs_ref.1, bf16[48,768]{1,0:T(8,128)(2,1)} %bitcast.16), custom_call_target="tpu_custom_call" | custom-call | flops 1000000000 | bytes 5000000 | tf_op jit(solution)/shard_map/pallas_call | solution.py:256
  4.9 8.8 %all-to-all-start = ((f32[8,8,512]{2,1,0:T(8,128)}), f32[8,8,512]{2,1,0:T(8,128)S(1)}, u32[]{:S(2)}, u32[]{:S(2)}) async-start(f32[8,8,512]{2,1,0:T(8,128)} %shard_map.68), calls=%async_computation | async-start | bytes 262144 | tf_op jit(solution)/shard_map/all_to_all | solution.py:271
  13.7 0.0 copy-done.5
  13.7 0.0 copy-start.4
  13.7 6.1 %shard_map.69 = (bf16[8,1024,256]{2,1,0:T(8,128)(2,1)}, f32[32,1024]{1,0:T(8,128)S(1)}) custom-call(bf16[512,32,128]{2,1,0:T(8,128)(2,1)} %bitcast.14, bf16[32,2048]{1,0:T(8,128)(2,1)S(1)} %bitcast.12), custom_call_target="tpu_custom_call" | custom-call | flops 4000000000 | bytes 9000000 | tf_op jit(solution)/shard_map/pallas_call | solution.py:272
  19.8 0.0 copy-start.2
  19.8 0.6 copy-done.2
  20.5 0.0 all-to-all-done.got_ref
  20.5 0.7 shard_map.70
  21.1 5.1 %all-to-all-start.1 = ((f32[8,8,512]{2,1,0:T(8,128)}), f32[8,8,512]{2,1,0:T(8,128)}, u32[]{:S(2)}, u32[]{:S(2)}) async-start(f32[8,8,512]{2,1,0:T(8,128)} %shard_map.70), calls=%async_computation.1 | async-start | bytes 262144 | tf_op jit(solution)/shard_map/all_to_all | solution.py:290
  26.3 0.0 copy-done.4
  26.3 0.1 copy.11
  26.4 0.2 reshape.26.ids_ref
  26.6 0.0 copy-start
  26.6 2.2 %copy-done = bf16[8,1024,256]{2,1,0:T(8,128)(2,1)S(1)} copy-done((bf16[8,1024,256]{2,1,0:T(8,128)(2,1)S(1)}, bf16[8,1024,256]{2,1,0:T(8,128)(2,1)}, u32[]{:S(2)}) %copy-start) | copy-done | bytes 4194328
  28.8 0.0 copy-start.3
  28.8 0.9 copy-done.3
  29.7 1.9 %shard_map.71.partly_ref = f32[64,104,128]{2,1,0:T(8,128)S(1)} custom-call(s32[64]{0:T(128)S(1)} %broadcast_select_fusion.place_ref, f32[8,8,512]{2,1,0:T(8,128)S(1)} %all-to-all-done.got_ref, f32[32,1024]{1,0:T(8,128)S(1)} %copy-done.3, s32[1,1024]{1,0:T(1,128)S(1)} %reshape.26.ids_ref, bf16[8,1024,256]{2,1,0:T(8,128)(2,1)S(1)} %copy-done), custom_call_target="tpu_custom_call" | custom-call | flops 1000000000 | bytes 6000000 | tf_op jit(solution)/shard_map/pallas_call | solution.py:291
  31.7 0.4 all-to-all-done.1.everyone_ref
  32.0 0.0 copy-start.1
  32.0 1.1 %copy-done.1 = bf16[512,768]{1,0:T(8,128)(2,1)S(1)} copy-done((bf16[512,768]{1,0:T(8,128)(2,1)S(1)}, bf16[512,768]{1,0:T(8,128)(2,1)}, u32[]{:S(2)}) %copy-start.1) | copy-done | bytes 786456
  33.2 1.6 %shard_map.72 = f32[64,104,128]{2,1,0:T(8,128)S(1)} custom-call(s32[64]{0:T(128)S(1)} %broadcast_select_fusion.place_ref, f32[8,8,512]{2,1,0:T(8,128)} %all-to-all-done.1.everyone_ref, s32[2,512]{1,0:T(2,128)S(1)} %bitcast.11, bf16[512,768]{1,0:T(8,128)(2,1)S(1)} %copy-done.1, f32[64,104,128]{2,1,0:T(8,128)S(1)} %shard_map.71.partly_ref), custom_call_target="tpu_custom_call", output_to_operand_aliasing={{}: (4, {})} | custom-call | flops 1000000000 | bytes 3000000 | tf_op jit(solution)/shard_map/pallas_call | solution.py:299
  34.8 26.1 %all_to_all.25 = f32[4,16,104,128]{3,2,1,0:T(8,128)S(1)} all-to-all(f32[4,16,104,128]{3,2,1,0:T(8,128)S(1)} %bitcast.10), channel_id=1, replica_groups={{0,128,256,384},{8,136,264,392},{16,144,272,400},{24,152,280,408},{1,9,..., dimensions={0} | all-to-all | bytes 6815744 | tf_op jit(solution)/shard_map/all_to_all | solution.py:44
  60.8 0.2 fusion
  61.0 12.9 %all_to_all.26 = f32[4,4,104,128]{3,2,1,0:T(8,128)S(1)} all-to-all(f32[4,4,104,128]{3,2,1,0:T(8,128)S(1)} %bitcast.15), channel_id=1, replica_groups={{0,8,16,24},{128,136,144,152},{256,264,272,280},{384,392,400,408},{1,12..., dimensions={0} | all-to-all | bytes 1703936 | tf_op jit(solution)/shard_map/all_to_all | solution.py:44
  73.9 29.6 %all_to_all.27.block_ref = f32[4,104,128]{2,1,0:T(8,128)S(1)} all-to-all(f32[4,104,128]{2,1,0:T(8,128)S(1)} %reduce_sum.9), channel_id=1, replica_groups={{0,32,64,96},{1,33,65,97},{2,34,66,98},{3,35,67,99},{4,36,68,100},{5,37..., dimensions={0} | all-to-all | bytes 425984 | tf_op jit(solution)/shard_map/all_to_all | solution.py:44
  103.5 0.7 shard_map.73
  (2 shorter events, 0.1 us)
Async XLA Ops:
  0.6 13.0 %copy-start.5 = (bf16[2048,32]{0,1:T(8,128)(2,1)S(1)}, bf16[2048,32]{0,1:T(8,128)(2,1)}, u32[]{:S(2)}) copy-start(bf16[2048,32]{0,1:T(8,128)(2,1)} %param.9) | copy-start | bytes 393220
  4.9 15.5 %all-to-all-start = ((f32[8,8,512]{2,1,0:T(8,128)}), f32[8,8,512]{2,1,0:T(8,128)S(1)}, u32[]{:S(2)}, u32[]{:S(2)}) async-start(f32[8,8,512]{2,1,0:T(8,128)} %shard_map.68), calls=%async_computation | async-start | bytes 262144 | tf_op jit(solution)/shard_map/all_to_all | solution.py:271
  13.7 12.6 %copy-start.4 = (s32[512,2]{0,1:T(2,128)S(1)}, s32[512,2]{0,1:T(2,128)}, u32[]{:S(2)}) copy-start(s32[512,2]{0,1:T(2,128)} %param.6) | copy-start | bytes 12292
  19.8 0.6 copy-start.2
  21.1 10.9 %all-to-all-start.1 = ((f32[8,8,512]{2,1,0:T(8,128)}), f32[8,8,512]{2,1,0:T(8,128)}, u32[]{:S(2)}, u32[]{:S(2)}) async-start(f32[8,8,512]{2,1,0:T(8,128)} %shard_map.70), calls=%async_computation.1 | async-start | bytes 262144 | tf_op jit(solution)/shard_map/all_to_all | solution.py:290
  26.6 2.2 %copy-start = (bf16[8,1024,256]{2,1,0:T(8,128)(2,1)S(1)}, bf16[8,1024,256]{2,1,0:T(8,128)(2,1)}, u32[]{:S(2)}) copy-start(bf16[8,1024,256]{2,1,0:T(8,128)(2,1)} %get-tuple-element.9.rows_ref) | copy-start | bytes 12582916
  28.8 0.9 copy-start.3
  32.0 1.1 %copy-start.1 = (bf16[512,768]{1,0:T(8,128)(2,1)S(1)}, bf16[512,768]{1,0:T(8,128)(2,1)}, u32[]{:S(2)}) copy-start(bf16[512,768]{1,0:T(8,128)(2,1)} %inputs_ref.1) | copy-start | bytes 2359300

commit v5 on v4

--- a/solution.py
+++ b/solution.py
@@ -26,7 +26,7 @@
     groups = []
     for zh in range(4):
         for t in range(8):
-            along_x = (t % 2 == 0) == first
+            along_x = (t % 2 == 1) == first
             for other in range(4):
                 groups.append(
                     [linear(i, zh, other, t) if along_x else linear(other, zh, i, t) for i in range(4)]
@@ -246,7 +246,7 @@
     core = lax.axis_index("tensor") % 2
     dp = jnp.arange(64, dtype=jnp.int32)
     x, zh, y = dp // 16, dp // 4 % 4, dp % 4
-    place = jnp.where(core == 0, (x * 4 + y) * 4 + zh, (y * 4 + x) * 4 + zh)
+    place = jnp.where(core == 1, (x * 4 + y) * 4 + zh, (y * 4 + x) * 4 + zh)
     bf16 = jnp.bfloat16
     ids_pair = expert_ids.T
     ids_row = expert_ids.reshape(1, 2 * tokens)

time: 105 us -> 105 us (level)
  no operation moved by 1% of the time
where the time goes in v5:
time: 105 us; the launch traced here: 104 us
  blocking collectives  68.5 us (65%)
  Pallas kernels  15.3 us (15%)
  starting transfers between devices  13.9 us (13%)
  local copies, waits for them, and re-layouts  5.19 us (5%)
    all_to_all x3, blocking collectives, swap(): return lax.all_to_all(block, AXES, 0, 0, axis_index_groups=groups)  68.5 us
    all_to_all x1, starting transfers between devices, body(): got = lax.all_to_all(send, 'tensor', 0, 0)  8.77 us
    pallas_call x1, Pallas kernels, body(): call(grads_kernel, (jax.ShapeDtypeStruct((8, 2 * tokens, 256), bf16), sha...  6.12 us
    all_to_all x1, starting transfers between devices, body(): everyone = lax.all_to_all(send, 'tensor', 0, 0)  5.12 us
    unnamed x13, local copies, waits for them, and re-layouts  5.01 us
    pallas_call x1, Pallas kernels, body(): call(norm_kernel, shape(8, 8, tokens), [HBM] * 3, VMEM, 10 ** 9, 5 * 10 *...  4.26 us
  transfers between devices with their start and end apart: 2, of which 1 were waited for; matrix products, arithmetic and copies ran while one was open for 0% of the time, Pallas kernels for 8%

profile of v5, /device:TPU:32, one launch (start us, length us, event | category | flops | bytes accessed | tf_op | source)
XLA Modules:
  0.0 104.2 jit_solution(17347023823016738277)
XLA Ops:
  0.6 0.0 copy-start.5
  0.6 4.3 %shard_map.68 = f32[8,8,512]{2,1,0:T(8,128)} custom-call(bf16[512,32,128]{2,1,0:T(8,128)(2,1)} %bitcast.13, bf16[512,768]{1,0:T(8,128)(2,1)} %inputs_ref.1, bf16[48,768]{1,0:T(8,128)(2,1)} %bitcast.16), custom_call_target="tpu_custom_call" | custom-call | flops 1000000000 | bytes 5000000 | tf_op jit(solution)/shard_map/pallas_call | solution.py:256
  4.9 8.8 %all-to-all-start = ((f32[8,8,512]{2,1,0:T(8,128)}), f32[8,8,512]{2,1,0:T(8,128)S(1)}, u32[]{:S(2)}, u32[]{:S(2)}) async-start(f32[8,8,512]{2,1,0:T(8,128)} %shard_map.68), calls=%async_computation | async-start | bytes 262144 | tf_op jit(solution)/shard_map/all_to_all | solution.py:271
  13.7 0.0 copy-done.5
  13.7 0.0 copy-start.4
  13.7 6.1 %shard_map.69 = (bf16[8,1024,256]{2,1,0:T(8,128)(2,1)}, f32[32,1024]{1,0:T(8,128)S(1)}) custom-call(bf16[512,32,128]{2,1,0:T(8,128)(2,1)} %bitcast.14, bf16[32,2048]{1,0:T(8,128)(2,1)S(1)} %bitcast.12), custom_call_target="tpu_custom_call" | custom-call | flops 4000000000 | bytes 9000000 | tf_op jit(solution)/shard_map/pallas_call | solution.py:272
  19.8 0.0 copy-start.2
  19.8 0.6 copy-done.2
  20.5 0.0 all-to-all-done.got_ref
  20.5 0.7 shard_map.70
  21.1 5.1 %all-to-all-start.1 = ((f32[8,8,512]{2,1,0:T(8,128)}), f32[8,8,512]{2,1,0:T(8,128)}, u32[]{:S(2)}, u32[]{:S(2)}) async-start(f32[8,8,512]{2,1,0:T(8,128)} %shard_map.70), calls=%async_computation.1 | async-start | bytes 262144 | tf_op jit(solution)/shard_map/all_to_all | solution.py:290
  26.3 0.0 copy-done.4
  26.3 0.1 copy.11
  26.4 0.2 reshape.26.ids_ref
  26.6 0.0 copy-start
  26.6 2.2 %copy-done = bf16[8,1024,256]{2,1,0:T(8,128)(2,1)S(1)} copy-done((bf16[8,1024,256]{2,1,0:T(8,128)(2,1)S(1)}, bf16[8,1024,256]{2,1,0:T(8,128)(2,1)}, u32[]{:S(2)}) %copy-start) | copy-done | bytes 4194328
  28.8 0.0 copy-start.3
  28.8 0.9 copy-done.3
  29.7 1.9 %shard_map.71.partly_ref = f32[64,104,128]{2,1,0:T(8,128)S(1)} custom-call(s32[64]{0:T(128)S(1)} %broadcast_select_fusion.place_ref, f32[8,8,512]{2,1,0:T(8,128)S(1)} %all-to-all-done.got_ref, f32[32,1024]{1,0:T(8,128)S(1)} %copy-done.3, s32[1,1024]{1,0:T(1,128)S(1)} %reshape.26.ids_ref, bf16[8,1024,256]{2,1,0:T(8,128)(2,1)S(1)} %copy-done), custom_call_target="tpu_custom_call" | custom-call | flops 1000000000 | bytes 6000000 | tf_op jit(solution)/shard_map/pallas_call | solution.py:291
  31.7 0.4 all-to-all-done.1.everyone_ref
  32.0 0.0 copy-start.1
  32.0 1.1 %copy-done.1 = bf16[512,768]{1,0:T(8,128)(2,1)S(1)} copy-done((bf16[512,768]{1,0:T(8,128)(2,1)S(1)}, bf16[512,768]{1,0:T(8,128)(2,1)}, u32[]{:S(2)}) %copy-start.1) | copy-done | bytes 786456
  33.2 1.6 %shard_map.72 = f32[64,104,128]{2,1,0:T(8,128)S(1)} custom-call(s32[64]{0:T(128)S(1)} %broadcast_select_fusion.place_ref, f32[8,8,512]{2,1,0:T(8,128)} %all-to-all-done.1.everyone_ref, s32[2,512]{1,0:T(2,128)S(1)} %bitcast.11, bf16[512,768]{1,0:T(8,128)(2,1)S(1)} %copy-done.1, f32[64,104,128]{2,1,0:T(8,128)S(1)} %shard_map.71.partly_ref), custom_call_target="tpu_custom_call", output_to_operand_aliasing={{}: (4, {})} | custom-call | flops 1000000000 | bytes 3000000 | tf_op jit(solution)/shard_map/pallas_call | solution.py:299
  34.8 26.1 %all_to_all.25 = f32[4,16,104,128]{3,2,1,0:T(8,128)S(1)} all-to-all(f32[4,16,104,128]{3,2,1,0:T(8,128)S(1)} %bitcast.10), channel_id=1, replica_groups={{0,8,16,24},{128,136,144,152},{256,264,272,280},{384,392,400,408},{1,12..., dimensions={0} | all-to-all | bytes 6815744 | tf_op jit(solution)/shard_map/all_to_all | solution.py:44
  60.8 0.2 fusion
  61.0 12.9 %all_to_all.26 = f32[4,4,104,128]{3,2,1,0:T(8,128)S(1)} all-to-all(f32[4,4,104,128]{3,2,1,0:T(8,128)S(1)} %bitcast.15), channel_id=1, replica_groups={{0,128,256,384},{8,136,264,392},{16,144,272,400},{24,152,280,408},{1,9,..., dimensions={0} | all-to-all | bytes 1703936 | tf_op jit(solution)/shard_map/all_to_all | solution.py:44
  73.9 29.6 %all_to_all.27.block_ref = f32[4,104,128]{2,1,0:T(8,128)S(1)} all-to-all(f32[4,104,128]{2,1,0:T(8,128)S(1)} %reduce_sum.9), channel_id=1, replica_groups={{0,32,64,96},{1,33,65,97},{2,34,66,98},{3,35,67,99},{4,36,68,100},{5,37..., dimensions={0} | all-to-all | bytes 425984 | tf_op jit(solution)/shard_map/all_to_all | solution.py:44
  103.5 0.7 shard_map.73
  (2 shorter events, 0.1 us)
Async XLA Ops:
  0.6 13.0 %copy-start.5 = (bf16[2048,32]{0,1:T(8,128)(2,1)S(1)}, bf16[2048,32]{0,1:T(8,128)(2,1)}, u32[]{:S(2)}) copy-start(bf16[2048,32]{0,1:T(8,128)(2,1)} %param.9) | copy-start | bytes 393220
  4.9 15.5 %all-to-all-start = ((f32[8,8,512]{2,1,0:T(8,128)}), f32[8,8,512]{2,1,0:T(8,128)S(1)}, u32[]{:S(2)}, u32[]{:S(2)}) async-start(f32[8,8,512]{2,1,0:T(8,128)} %shard_map.68), calls=%async_computation | async-start | bytes 262144 | tf_op jit(solution)/shard_map/all_to_all | solution.py:271
  13.7 12.6 %copy-start.4 = (s32[512,2]{0,1:T(2,128)S(1)}, s32[512,2]{0,1:T(2,128)}, u32[]{:S(2)}) copy-start(s32[512,2]{0,1:T(2,128)} %param.6) | copy-start | bytes 12292
  19.8 0.6 copy-start.2
  21.1 10.9 %all-to-all-start.1 = ((f32[8,8,512]{2,1,0:T(8,128)}), f32[8,8,512]{2,1,0:T(8,128)}, u32[]{:S(2)}, u32[]{:S(2)}) async-start(f32[8,8,512]{2,1,0:T(8,128)} %shard_map.70), calls=%async_computation.1 | async-start | bytes 262144 | tf_op jit(solution)/shard_map/all_to_all | solution.py:290
  26.6 2.2 %copy-start = (bf16[8,1024,256]{2,1,0:T(8,128)(2,1)S(1)}, bf16[8,1024,256]{2,1,0:T(8,128)(2,1)}, u32[]{:S(2)}) copy-start(bf16[8,1024,256]{2,1,0:T(8,128)(2,1)} %get-tuple-element.9.rows_ref) | copy-start | bytes 12582916
  28.8 0.9 copy-start.3
  32.0 1.1 %copy-start.1 = (bf16[512,768]{1,0:T(8,128)(2,1)S(1)}, bf16[512,768]{1,0:T(8,128)(2,1)}, u32[]{:S(2)}) copy-start(bf16[512,768]{1,0:T(8,128)(2,1)} %inputs_ref.1) | copy-start | bytes 2359300
